TPU v7x, 32 devices: a whole 2x2x4 slice. The times are simulated.
32 devices in a mesh: groups: 2 (over x), gx: 8 (over z, y), gy: 2 (over core).
Axes of the slice: x: 2, y: 2, z: 4, core: 2. Of those that a mesh axis runs over, the one named last changes fastest.
Arguments:
- tokens: bfloat16 [16, 14336], P(('groups', 'gy'), 'gx'), parts along dimension 0, may hold values from -6 to 6
- gate_weight: bfloat16 [14336, 26624], P('gx', 'gy'), may hold values from -0.046875 to 0.046875
- up_weight: bfloat16 [14336, 26624], P('gx', 'gy'), may hold values from -0.046875 to 0.046875
Outputs:
- hidden: bfloat16 [16, 26624], P(('groups', 'gx'), 'gy'), parts along dimension 0
There are 2 independent parts, one for each index of `groups`. A program takes and returns all parts, laid end to end along the dimension named above; an argument that names none is the same for every part. Nothing has to cross between parts.
All inputs are finite; a program needn't handle non-finite values.
Results may differ from a plain program's by a relative error of at most 0.001.
Values may be sent and summed in bfloat16 or wider, within the bound.
No kernel may reach another device: no remote copies, remote signals or barrier semaphores. Data moves between devices by JAX's collectives and lax.ppermute only.
A program may use at most 192 MiB of HBM per device.

v0:
```python
import jax
import jax.numpy as jnp
from jax import lax
from jax.sharding import PartitionSpec as P


def per_device(tokens, gate_weight, up_weight):
    rows_all = lax.all_gather(tokens, "gy", axis=0, tiled=True)
    block = rows_all
    gate = lax.psum_scatter(
        jnp.dot(block, gate_weight, preferred_element_type=jnp.float32),
        "gx",
        scatter_dimension=0,
        tiled=True,
    )
    block = rows_all
    up = lax.psum_scatter(
        jnp.dot(block, up_weight, preferred_element_type=jnp.float32),
        "gx",
        scatter_dimension=0,
        tiled=True,
    )
    return (jax.nn.silu(gate) * up).astype(jnp.bfloat16)


def solution(mesh):
    in_specs = (P(("groups", "gy"), "gx"), P("gx", "gy"), P("gx", "gy"))
    out_specs = P(("groups", "gx"), "gy")
    return jax.shard_map(
        per_device, mesh=mesh, in_specs=in_specs, out_specs=out_specs, check_vma=False
    )
```

profile of v0, /device:TPU:0, one launch (start us, length us, event | category | flops | bytes accessed | tf_op | source)
XLA Modules:
  0.0 133.6 jit_solution(11298429839037707297)
XLA Ops:
  6.5 0.0 all-reduce.5.cloned.1.call-start
  6.5 2.1 %all-gather = bf16[2,4,1792]{2,1,0:T(4,128)(2,1)S(1)} all-gather(bf16[1,4,1792]{2,1,0:T(4,128)(2,1)} %bitcast.6), channel_id=1, replica_groups=mesh['groups'=2,'gx'=8,'gy'=2] {'gy'}, dimensions={0}, use_global_device_ids=true | all-gather | bytes 43008 | tf_op jit(solution)/shard_map/all_gather | solution.py:8
  8.7 0.0 copy-start
  8.7 18.6 %fusion.2 = f32[8,13312]{1,0:T(8,128)} fusion(bf16[8,1792]{1,0:T(8,128)(2,1)S(1)} %reshape.1, bf16[1792,13312]{1,0:T(8,128)(2,1)} %param.4), kind=kOutput, calls=%fused_computation.3 | convolution fusion | flops 381681664 | bytes 48164864 | tf_op jit(solution)/shard_map/dot_general | solution.py:11
  27.3 18.5 %fusion.3 = f32[8,13312]{1,0:T(8,128)} fusion(bf16[8,1792]{1,0:T(8,128)(2,1)S(1)} %reshape.1, bf16[1792,13312]{1,0:T(8,128)(2,1)} %param.5), kind=kOutput, calls=%fused_computation.4 | convolution fusion | flops 381681664 | bytes 48164864 | tf_op jit(solution)/shard_map/dot_general | solution.py:18
  45.8 0.0 all-reduce.5.cloned.1.call-update
  45.9 0.0 copy-done
  45.9 0.6 dynamic-slice
  46.5 77.7 %all-reduce.5.cloned.1.call-done = (f32[8,13312]{1,0:T(8,128)}, f32[8,13312]{1,0:T(8,128)}) async-done(((f32[8,13312]{1,0:T(8,128)}, f32[8,13312]{1,0:T(8,128)}), (f32[8,13312]{1,0:T(8,128)}, f32[8,13312]{1,0:T(8,128)})) %all-reduce.5.cloned.1.call-update) | async-done | bytes 851984
  124.2 2.6 %fusion.1 = bf16[1,13312]{1,0:T(2,128)(2,1)} fusion(f32[8,13312]{1,0:T(8,128)} %get-tuple-element.5, u32[]{:T(128)} %bitcast.1, f32[8,13312]{1,0:T(8,128)} %get-tuple-element.6), kind=kLoop, calls=%fused_computation.2 | loop fusion | flops 79872 | bytes 133124 | tf_op jit(solution)/shard_map/convert_element_type | solution.py:23
  (1 shorter events, 0.0 us)
Async XLA Ops:
  6.5 117.6 %all-reduce.5.cloned.1.call-start = ((), (), s32[]{:S(2)}) async-start(), calls=%async_computation | async-start | bytes 1703936
  8.7 37.2 %copy-start = (u32[32]{0:T(128)S(1)}, u32[32]{0:T(128)}, u32[]{:S(2)}) copy-start(u32[32]{0:T(128)} %constant.5) | copy-start | bytes 388
Sparse Core Ops, SparseCore 0:
  46.0 78.1 all-reduce.4
where the time goes:
time: 134 us
  waiting for transfers between devices  77.7 us (58%)
  matrix products  37.1 us (28%)
  between operations  13.4 us (10%)
  other arithmetic  2.56 us (2%)
  blocking collectives  2.14 us (2%)
    unnamed x2, waiting for transfers between devices  77.7 us
    dot_general x1, matrix products, per_device(): jnp.dot(block, gate_weight, preferred_element_type=jnp.float32)  18.6 us
    dot_general x1, matrix products, per_device(): jnp.dot(block, up_weight, preferred_element_type=jnp.float32)  18.5 us
  transfers between devices with their start and end apart: 1, of which 1 were waited for; matrix products, arithmetic and copies ran while one was open for 0% of the time, Pallas kernels for 0%

commit v1 on v0

v1 whole, which is shorter than its diff:
```python
import functools

import jax
import jax.numpy as jnp
from jax import lax
from jax.experimental import pallas as pl
from jax.experimental.pallas import tpu as pltpu
from jax.sharding import PartitionSpec as P

LANES = 128


def masks(count, core):
    bits = [1 << b for b in range(count.bit_length() - 1)]
    if core % 2 and len(bits) > 1:
        bits[0], bits[1] = bits[1], bits[0]
    return bits


def column_block(width):
    units = width // LANES
    return LANES * max(d for d in range(1, min(units, 4) + 1) if units % d == 0)


def project_kernel(sizes, base_blocks, block, blocks, tokens_ref, gate_hbm, up_hbm, send_ref, keep_ref, rows_ref, buffer, sems):
    groups, gx, gy = sizes
    group, x, core = lax.axis_index("groups"), lax.axis_index("gx"), lax.axis_index("gy")
    base = group * base_blocks
    slots = buffer.shape[0]

    def copies(i, slot):
        columns = pl.ds(pl.multiple_of((base + i) * block, LANES), block)
        return [
            pltpu.make_async_copy(hbm.at[:, columns], buffer.at[slot, w], sems.at[slot, w])
            for w, hbm in enumerate((gate_hbm, up_hbm))
        ]

    for i in range(min(slots - 1, blocks)):
        for copy in copies(i, i):
            copy.start()

    rows = tokens_ref.shape[0]
    each = rows // (groups * gx)
    m = lax.broadcasted_iota(jnp.int32, (rows, rows), 0)
    source = lax.broadcasted_iota(jnp.int32, (rows, rows), 1)
    j, q, i = m // (groups * each), (m // each) % groups, m % each
    mine, other = masks(gx, 0), masks(gx, 1)
    flip = jnp.zeros_like(j)
    for n in range(len(mine)):
        bit = (j // (1 << (len(mine) - 1 - n))) % 2
        flip = flip + bit * jnp.where(core == 0, mine[n], other[n])
    wanted = ((group + q) % groups) * (gx * each) + (x ^ flip) * each + i
    pick = (source == wanted).astype(jnp.bfloat16)
    rows_ref[...] = jnp.dot(pick, tokens_ref[...], preferred_element_type=jnp.float32).astype(jnp.bfloat16)

    half = rows // 2

    def step(n, carry):
        slot = lax.rem(n, slots)

        @pl.when(n + slots - 1 < blocks)
        def _():
            for copy in copies(n + slots - 1, lax.rem(n + slots - 1, slots)):
                copy.start()

        columns = pl.ds(pl.multiple_of(n * block, LANES), block)
        for w, copy in enumerate(copies(n, slot)):
            copy.wait()
            total = jnp.dot(rows_ref[...], buffer[slot, w], preferred_element_type=jnp.float32)
            keep_ref[w, :, columns] = total[:half]
            send_ref[w, :, columns] = total[half:]
        return carry

    lax.fori_loop(0, blocks, step, 0)


def project(sizes, tokens, gate_weight, up_weight):
    rows, depth = tokens.shape
    width = gate_weight.shape[1] // sizes[0]
    block = column_block(width)
    blocks = width // block
    slots = min(4, blocks)
    shape = jax.ShapeDtypeStruct((2, rows // 2, width), jnp.float32)
    return pl.pallas_call(
        functools.partial(project_kernel, sizes, blocks, block, blocks),
        in_specs=[
            pl.BlockSpec(memory_space=pltpu.VMEM),
            pl.BlockSpec(memory_space=pl.ANY),
            pl.BlockSpec(memory_space=pl.ANY),
        ],
        out_specs=[pl.BlockSpec(memory_space=pltpu.VMEM)] * 2,
        out_shape=[shape, shape],
        scratch_shapes=[
            pltpu.VMEM((rows, depth), jnp.bfloat16),
            pltpu.VMEM((slots, 2, depth, block), jnp.bfloat16),
            pltpu.SemaphoreType.DMA((slots, 2)),
        ],
        cost_estimate=pl.CostEstimate(
            flops=4 * rows * depth * width, bytes_accessed=4 * depth * width, transcendentals=0
        ),
        compiler_params=pltpu.CompilerParams(vmem_limit_bytes=44 << 20),
    )(tokens, gate_weight, up_weight)


def per_device(sizes, tokens, gate_weight, up_weight):
    groups, gx, gy = sizes
    rows = lax.all_gather(tokens, ("groups", "gy"), axis=0, tiled=True)
    send, keep = project(sizes, rows, gate_weight, up_weight)
    phases = gx.bit_length() - 1
    for n in range(phases):
        pairs = [
            (x * gy + core, (x ^ masks(gx, core)[n]) * gy + core) for x in range(gx) for core in range(gy)
        ]
        total = keep + lax.ppermute(send, ("gx", "gy"), pairs)
        half = total.shape[1] // 2
        if n < phases - 1:
            keep, send = total[:, :half], total[:, half:]
    hidden = (jax.nn.silu(total[0]) * total[1]).astype(jnp.bfloat16)
    each = hidden.shape[0] // groups
    own, theirs = hidden[:each], hidden[each:]
    theirs = lax.ppermute(theirs, "groups", [(g, (g + 1) % groups) for g in range(groups)])
    first = lax.axis_index("groups") == 0
    return jnp.concatenate([jnp.where(first, own, theirs), jnp.where(first, theirs, own)], axis=1)


def solution(mesh):
    sizes = tuple(mesh.shape[name] for name in ("groups", "gx", "gy"))
    in_specs = (P(("groups", "gy"), "gx"), P("gx", "gy"), P("gx", "gy"))
    out_specs = P(("groups", "gx"), "gy")
    return jax.shard_map(
        functools.partial(per_device, sizes), mesh=mesh, in_specs=in_specs, out_specs=out_specs, check_vma=False
    )
```

time: 134 us -> 48.2 us (0.36)
  waiting for transfers between devices: 77.7 us -> 14.7 us
  matrix products: 37.1 us -> 0 us
  Pallas kernels: 0 us -> 15.7 us
  between operations: 13.4 us -> 0.06 us
  starting transfers between devices: 0.01 us -> 10.1 us
  blocking collectives: 2.14 us -> 6.42 us
  other arithmetic: 2.56 us -> 0.97 us
    unnamed x2 -> x0, waiting for transfers between devices: 77.7 us -> none
    dot_general x2 -> x0, matrix products: 37.1 us -> none  [the longest x1 18.6 us: per_device(): jnp.dot(block, gate_weight, preferred_element_type=jnp.float32)]
    pallas_call x0 -> x1, Pallas kernels: none -> 15.7 us  [project(): pl.pallas_call(functools.partial(project_kernel, sizes, blocks, block, bl...]
    ppermute x0 -> x4, waiting for transfers between devices: none -> 14.7 us  [the longest x3 12.9 us: per_device(): total = keep + lax.ppermute(send, ('gx', 'gy'), pairs)]
    ppermute x0 -> x4, starting transfers between devices: none -> 10.1 us  [the longest x3 7.28 us: per_device(): total = keep + lax.ppermute(send, ('gx', 'gy'), pairs)]
    all_gather x1, blocking collectives: 2.14 us -> 6.42 us  [per_device(): rows = lax.all_gather(tokens, ('groups', 'gy'), axis=0, tiled=True)]
    convert_element_type x1, other arithmetic: 2.56 us -> 0.07 us  [per_device(): hidden = (jax.nn.silu(total[0]) * total[1]).astype(jnp.bfloat16)]
  transfers between devices with their start and end apart: 1 -> 4, of which waited for: 1 -> 4; matrix products, arithmetic and copies ran while one was open for 0% -> 0% of each run, Pallas kernels for 0% -> 0%
where the time goes in v1:
time: 48.2 us; the launch traced here: 48 us
  Pallas kernels  15.7 us (33%)
  waiting for transfers between devices  14.7 us (30%)
  starting transfers between devices  10.1 us (21%)
  blocking collectives  6.42 us (13%)
  other arithmetic  0.97 us (2%)
    pallas_call x1, Pallas kernels, project(): pl.pallas_call(functools.partial(project_kernel, sizes, blocks, block, bl...  15.7 us
    ppermute x3, waiting for transfers between devices, per_device(): total = keep + lax.ppermute(send, ('gx', 'gy'), pairs)  12.9 us
    ppermute x3, starting transfers between devices, per_device(): total = keep + lax.ppermute(send, ('gx', 'gy'), pairs)  7.28 us
    all_gather x1, blocking collectives, per_device(): rows = lax.all_gather(tokens, ('groups', 'gy'), axis=0, tiled=True)  6.42 us
    ppermute x1, starting transfers between devices, per_device(): lax.ppermute(theirs, 'groups', [(g, (g + 1) % groups) for g in range(grou...  2.8 us
    ppermute x1, waiting for transfers between devices, per_device(): lax.ppermute(theirs, 'groups', [(g, (g + 1) % groups) for g in range(grou...  1.83 us
  transfers between devices with their start and end apart: 4, of which 4 were waited for; matrix products, arithmetic and copies ran while one was open for 0% of the time, Pallas kernels for 0%

profile of v1, /device:TPU:0, one launch (start us, length us, event | category | flops | bytes accessed | tf_op | source)
XLA Modules:
  0.0 48.0 jit_solution(15542946042910344942)
XLA Ops:
  0.0 6.4 %all-gather = bf16[4,4,1792]{2,1,0:T(4,128)(2,1)S(1)} all-gather(bf16[1,4,1792]{2,1,0:T(4,128)(2,1)} %bitcast.13), channel_id=1, replica_groups=mesh['groups'=2,'gx'=8,'gy'=2] {'groups','gy'}, dimensions={0}, use_global_device_ids=true | all-gather | bytes 71680 | tf_op jit(solution)/shard_map/all_gather | solution.py:107
  6.4 15.7 %shard_map.37 = (f32[2,8,6656]{2,1,0:T(8,128)S(1)}, f32[2,8,6656]{2,1,0:T(8,128)S(1)}) custom-call(bf16[16,1792]{1,0:T(8,128)(2,1)S(1)} %reshape.1.tokens_ref, bf16[1792,13312]{1,0:T(8,128)(2,1)} %gate_hbm.1, bf16[1792,13312]{1,0:T(8,128)(2,1)} %up_hbm.1), custom_call_target="tpu_custom_call" | custom-call | flops 763363328 | bytes 47710208 | tf_op jit(solution)/shard_map/pallas_call | solution.py:84
  22.1 2.1 %collective-permute-start = (f32[2,8,6656]{2,1,0:T(8,128)S(1)}, f32[2,8,6656]{2,1,0:T(8,128)S(1)}, u32[]{:S(2)}, u32[]{:S(2)}) collective-permute-start(f32[2,8,6656]{2,1,0:T(8,128)S(1)} %get-tuple-element.8), channel_id=1, source_target_pairs={{0,2},{1,5},{2,0},{3,7},{4,6},{5,1},{6,4},{7,3},{8,10},{9,13},{10,... | collective-permute-start | bytes 1277960 | tf_op jit(solution)/shard_map/ppermute | solution.py:114
  24.2 6.1 %collective-permute-done = f32[2,8,6656]{2,1,0:T(8,128)S(1)} collective-permute-done((f32[2,8,6656]{2,1,0:T(8,128)S(1)}, f32[2,8,6656]{2,1,0:T(8,128)S(1)}, u32[]{:S(2)}, u32[]{:S(2)}) %collective-permute-start) | collective-permute-done | bytes 426016 | tf_op jit(solution)/shard_map/ppermute | solution.py:114
  30.3 0.1 add.13
  30.4 2.1 %collective-permute-start.1 = (f32[2,4,6656]{2,1,0:T(4,128)S(1)}, f32[2,4,6656]{2,1,0:T(4,128)S(1)}, u32[]{:S(2)}, u32[]{:S(2)}) collective-permute-start(f32[2,4,6656]{2,1,0:T(4,128)S(1)} %slice.33), channel_id=1, source_target_pairs={{0,4},{1,3},{2,6},{3,1},{4,0},{5,7},{6,2},{7,5},{8,12},{9,11},{10,... | collective-permute-start | bytes 638984 | tf_op jit(solution)/shard_map/ppermute | solution.py:114
  32.5 3.8 %collective-permute-done.1 = f32[2,4,6656]{2,1,0:T(4,128)S(1)} collective-permute-done((f32[2,4,6656]{2,1,0:T(4,128)S(1)}, f32[2,4,6656]{2,1,0:T(4,128)S(1)}, u32[]{:S(2)}, u32[]{:S(2)}) %collective-permute-start.1) | collective-permute-done | bytes 213024 | tf_op jit(solution)/shard_map/ppermute | solution.py:114
  36.4 0.1 slice.35
  36.5 3.1 %collective-permute-start.2 = (f32[2,2,6656]{2,1,0:T(2,128)S(1)}, f32[2,2,6656]{2,1,0:T(2,128)S(1)}, u32[]{:S(2)}, u32[]{:S(2)}) collective-permute-start(f32[2,2,6656]{2,1,0:T(2,128)S(1)} %slice.35), channel_id=1, source_target_pairs={{0,8},{1,9},{2,10},{3,11},{4,12},{5,13},{6,14},{7,15},{8,0},{9,1},... | collective-permute-start | bytes 319496 | tf_op jit(solution)/shard_map/ppermute | solution.py:114
  39.6 2.9 %collective-permute-done.2 = f32[2,2,6656]{2,1,0:T(2,128)S(1)} collective-permute-done((f32[2,2,6656]{2,1,0:T(2,128)S(1)}, f32[2,2,6656]{2,1,0:T(2,128)S(1)}, u32[]{:S(2)}, u32[]{:S(2)}) %collective-permute-start.2) | collective-permute-done | bytes 106528 | tf_op jit(solution)/shard_map/ppermute | solution.py:114
  42.5 0.1 slice_add_fusion.1
  42.5 0.1 fusion.1
  42.7 2.8 %collective-permute-start.3 = (bf16[1,6656]{1,0:T(2,128)(2,1)S(1)}, bf16[1,6656]{1,0:T(2,128)(2,1)S(1)}, u32[]{:S(2)}, u32[]{:S(2)}) collective-permute-start(bf16[1,6656]{1,0:T(2,128)(2,1)S(1)} %slice.39), channel_id=1, source_target_pairs={{0,16},{16,0},{1,17},{17,1},{2,18},{18,2},{3,19},{19,3},{4,20},{20... | collective-permute-start | bytes 39944 | tf_op jit(solution)/shard_map/ppermute | solution.py:121
  45.5 1.8 %collective-permute-done.3 = bf16[1,6656]{1,0:T(2,128)(2,1)S(1)} collective-permute-done((bf16[1,6656]{1,0:T(2,128)(2,1)S(1)}, bf16[1,6656]{1,0:T(2,128)(2,1)S(1)}, u32[]{:S(2)}, u32[]{:S(2)}) %collective-permute-start.3) | collective-permute-done | bytes 13344 | tf_op jit(solution)/shard_map/ppermute | solution.py:121
  47.3 0.1 broadcast_select_fusion.1
  47.3 0.7 %pad_maximum_fusion = bf16[1,13312]{1,0:T(2,128)(2,1)} fusion(bf16[1,6656]{1,0:T(2,128)(2,1)S(1)} %get-tuple-element.10, bf16[1,6656]{1,0:T(2,128)(2,1)S(1)} %get-tuple-element.9), kind=kLoop, calls=%fused_computation.6 | loop fusion | flops 53248 | bytes 53248 | tf_op jit(solution)/shard_map/concatenate | solution.py:123
  (4 shorter events, 0.1 us)
Async XLA Ops:
  22.1 8.2 %collective-permute-start = (f32[2,8,6656]{2,1,0:T(8,128)S(1)}, f32[2,8,6656]{2,1,0:T(8,128)S(1)}, u32[]{:S(2)}, u32[]{:S(2)}) collective-permute-start(f32[2,8,6656]{2,1,0:T(8,128)S(1)} %get-tuple-element.8), channel_id=1, source_target_pairs={{0,2},{1,5},{2,0},{3,7},{4,6},{5,1},{6,4},{7,3},{8,10},{9,13},{10,... | collective-permute-start | bytes 1277960 | tf_op jit(solution)/shard_map/ppermute | solution.py:114
  30.4 5.9 %collective-permute-start.1 = (f32[2,4,6656]{2,1,0:T(4,128)S(1)}, f32[2,4,6656]{2,1,0:T(4,128)S(1)}, u32[]{:S(2)}, u32[]{:S(2)}) collective-permute-start(f32[2,4,6656]{2,1,0:T(4,128)S(1)} %slice.33), channel_id=1, source_target_pairs={{0,4},{1,3},{2,6},{3,1},{4,0},{5,7},{6,2},{7,5},{8,12},{9,11},{10,... | collective-permute-start | bytes 638984 | tf_op jit(solution)/shard_map/ppermute | solution.py:114
  36.5 6.0 %collective-permute-start.2 = (f32[2,2,6656]{2,1,0:T(2,128)S(1)}, f32[2,2,6656]{2,1,0:T(2,128)S(1)}, u32[]{:S(2)}, u32[]{:S(2)}) collective-permute-start(f32[2,2,6656]{2,1,0:T(2,128)S(1)} %slice.35), channel_id=1, source_target_pairs={{0,8},{1,9},{2,10},{3,11},{4,12},{5,13},{6,14},{7,15},{8,0},{9,1},... | collective-permute-start | bytes 319496 | tf_op jit(solution)/shard_map/ppermute | solution.py:114
  42.7 4.6 %collective-permute-start.3 = (bf16[1,6656]{1,0:T(2,128)(2,1)S(1)}, bf16[1,6656]{1,0:T(2,128)(2,1)S(1)}, u32[]{:S(2)}, u32[]{:S(2)}) collective-permute-start(bf16[1,6656]{1,0:T(2,128)(2,1)S(1)} %slice.39), channel_id=1, source_target_pairs={{0,16},{16,0},{1,17},{17,1},{2,18},{18,2},{3,19},{19,3},{4,20},{20... | collective-permute-start | bytes 39944 | tf_op jit(solution)/shard_map/ppermute | solution.py:121

commit v2 on v1

--- a/solution.py
+++ b/solution.py
@@ -22,10 +22,27 @@
     return LANES * max(d for d in range(1, min(units, 4) + 1) if units % d == 0)
 
 
-def project_kernel(sizes, base_blocks, block, blocks, tokens_ref, gate_hbm, up_hbm, send_ref, keep_ref, rows_ref, buffer, sems):
+def pick_rows(sizes, tokens):
     groups, gx, gy = sizes
     group, x, core = lax.axis_index("groups"), lax.axis_index("gx"), lax.axis_index("gy")
-    base = group * base_blocks
+    rows = tokens.shape[0]
+    each = rows // (groups * gx)
+    m = lax.broadcasted_iota(jnp.int32, (rows, rows), 0)
+    source = lax.broadcasted_iota(jnp.int32, (rows, rows), 1)
+    j, q, i = m // (groups * each), (m // each) % groups, m % each
+    mine, other = masks(gx, 0), masks(gx, 1)
+    flip = jnp.zeros_like(j)
+    for n in range(len(mine)):
+        bit = (j // (1 << (len(mine) - 1 - n))) % 2
+        flip = flip + bit * jnp.where(core == 0, mine[n], other[n])
+    wanted = ((group + q) % groups) * (gx * each) + (x ^ flip) * each + i
+    pick = (source == wanted).astype(jnp.bfloat16)
+    return jnp.dot(pick, tokens, preferred_element_type=jnp.float32).astype(jnp.bfloat16)
+
+
+def project_kernel(sizes, all_blocks, part, block, first, tokens_ref, gate_hbm, up_hbm, send_ref, keep_ref, rows_ref, buffer, sems):
+    base = lax.axis_index("groups") * all_blocks + part[0]
+    blocks = part[1] - part[0]
     slots = buffer.shape[0]
 
     def copies(i, slot):
@@ -39,21 +56,8 @@
         for copy in copies(i, i):
             copy.start()
 
-    rows = tokens_ref.shape[0]
-    each = rows // (groups * gx)
-    m = lax.broadcasted_iota(jnp.int32, (rows, rows), 0)
-    source = lax.broadcasted_iota(jnp.int32, (rows, rows), 1)
-    j, q, i = m // (groups * each), (m // each) % groups, m % each
-    mine, other = masks(gx, 0), masks(gx, 1)
-    flip = jnp.zeros_like(j)
-    for n in range(len(mine)):
-        bit = (j // (1 << (len(mine) - 1 - n))) % 2
-        flip = flip + bit * jnp.where(core == 0, mine[n], other[n])
-    wanted = ((group + q) % groups) * (gx * each) + (x ^ flip) * each + i
-    pick = (source == wanted).astype(jnp.bfloat16)
-    rows_ref[...] = jnp.dot(pick, tokens_ref[...], preferred_element_type=jnp.float32).astype(jnp.bfloat16)
-
-    half = rows // 2
+    rows_ref[...] = pick_rows(sizes, tokens_ref[...]) if first else tokens_ref[...]
+    half = rows_ref.shape[0] // 2
 
     def step(n, carry):
         slot = lax.rem(n, slots)
@@ -74,24 +78,23 @@
     lax.fori_loop(0, blocks, step, 0)
 
 
-def project(sizes, tokens, gate_weight, up_weight):
+def project(sizes, part, block, first, tokens, gate_weight, up_weight):
     rows, depth = tokens.shape
-    width = gate_weight.shape[1] // sizes[0]
-    block = column_block(width)
-    blocks = width // block
+    all_blocks = gate_weight.shape[1] // (sizes[0] * block)
+    blocks = part[1] - part[0]
+    width = blocks * block
     slots = min(4, blocks)
     shape = jax.ShapeDtypeStruct((2, rows // 2, width), jnp.float32)
     return pl.pallas_call(
-        functools.partial(project_kernel, sizes, blocks, block, blocks),
+        functools.partial(project_kernel, sizes, all_blocks, part, block, first),
         in_specs=[
             pl.BlockSpec(memory_space=pltpu.VMEM),
             pl.BlockSpec(memory_space=pl.ANY),
             pl.BlockSpec(memory_space=pl.ANY),
         ],
-        out_specs=[pl.BlockSpec(memory_space=pltpu.VMEM)] * 2,
-        out_shape=[shape, shape],
+        out_specs=[pl.BlockSpec(memory_space=pltpu.VMEM)] * 3,
+        out_shape=[shape, shape, jax.ShapeDtypeStruct((rows, depth), jnp.bfloat16)],
         scratch_shapes=[
-            pltpu.VMEM((rows, depth), jnp.bfloat16),
             pltpu.VMEM((slots, 2, depth, block), jnp.bfloat16),
             pltpu.SemaphoreType.DMA((slots, 2)),
         ],
@@ -102,19 +105,35 @@
     )(tokens, gate_weight, up_weight)
 
 
+def exchange(sizes, n, send):
+    groups, gx, gy = sizes
+    pairs = [(x * gy + core, (x ^ masks(gx, core)[n]) * gy + core) for x in range(gx) for core in range(gy)]
+    return lax.ppermute(send, ("gx", "gy"), pairs)
+
+
+def halves(total):
+    half = total.shape[1] // 2
+    return total[:, half:], total[:, :half]
+
+
 def per_device(sizes, tokens, gate_weight, up_weight):
     groups, gx, gy = sizes
-    rows = lax.all_gather(tokens, ("groups", "gy"), axis=0, tiled=True)
-    send, keep = project(sizes, rows, gate_weight, up_weight)
+    tokens = lax.all_gather(tokens, ("groups", "gy"), axis=0, tiled=True)
+    width = gate_weight.shape[1] // groups
+    block = column_block(width)
+    blocks = width // block
+    cut = blocks * 9 // 13
     phases = gx.bit_length() - 1
-    for n in range(phases):
-        pairs = [
-            (x * gy + core, (x ^ masks(gx, core)[n]) * gy + core) for x in range(gx) for core in range(gy)
-        ]
-        total = keep + lax.ppermute(send, ("gx", "gy"), pairs)
-        half = total.shape[1] // 2
-        if n < phases - 1:
-            keep, send = total[:, :half], total[:, half:]
+    sums = []
+    for first, part in ((True, (0, cut)), (False, (cut, blocks))):
+        send, keep, tokens = project(sizes, part, block, first, tokens, gate_weight, up_weight)
+        send, keep = halves(keep + exchange(sizes, 0, send))
+        sums.append((send, keep))
+    sums = [keep + exchange(sizes, 1, send) for send, keep in sums]
+    total = jnp.concatenate(sums, axis=2)
+    for n in range(2, phases):
+        send, keep = halves(total)
+        total = keep + exchange(sizes, n, send)
     hidden = (jax.nn.silu(total[0]) * total[1]).astype(jnp.bfloat16)
     each = hidden.shape[0] // groups
     own, theirs = hidden[:each], hidden[each:]

time: 48.2 us -> 49.9 us (1.035)
  Pallas kernels: 15.7 us -> 17.5 us
  starting transfers between devices: 10.1 us -> 8.83 us
  waiting for transfers between devices: 14.7 us -> 15.8 us
    pallas_call x1 -> x2, Pallas kernels: 15.7 us -> 17.5 us  [project(): pl.pallas_call(functools.partial(project_kernel, sizes, all_blocks, part,...]
    ppermute x1, starting transfers between devices: 2.8 us -> 1.49 us  [per_device(): lax.ppermute(theirs, 'groups', [(g, (g + 1) % groups) for g in range(grou...]
    ppermute x1, waiting for transfers between devices: 1.83 us -> 2.42 us  [per_device(): lax.ppermute(theirs, 'groups', [(g, (g + 1) % groups) for g in range(grou...]
    ppermute x3 -> x5, waiting for transfers between devices: 12.9 us -> 13.4 us  [exchange(): return lax.ppermute(send, ('gx', 'gy'), pairs)]
    ppermute x3 -> x5, starting transfers between devices: 7.28 us -> 7.34 us  [exchange(): return lax.ppermute(send, ('gx', 'gy'), pairs)]
  transfers between devices with their start and end apart: 4 -> 6, of which waited for: 4 -> 5; matrix products, arithmetic and copies ran while one was open for 0% -> 0% of each run, Pallas kernels for 0% -> 12%
where the time goes in v2:
time: 49.9 us; the launch traced here: 49.8 us
  Pallas kernels  17.5 us (35%)
  waiting for transfers between devices  15.8 us (32%)
  starting transfers between devices  8.83 us (18%)
  blocking collectives  6.42 us (13%)
  other arithmetic  1.05 us (2%)
    pallas_call x2, Pallas kernels, project(): pl.pallas_call(functools.partial(project_kernel, sizes, all_blocks, part,...  17.5 us
    ppermute x5, waiting for transfers between devices, exchange(): return lax.ppermute(send, ('gx', 'gy'), pairs)  13.4 us
    ppermute x5, starting transfers between devices, exchange(): return lax.ppermute(send, ('gx', 'gy'), pairs)  7.34 us
    all_gather x1, blocking collectives, per_device(): tokens = lax.all_gather(tokens, ('groups', 'gy'), axis=0, tiled=True)  6.42 us
    ppermute x1, waiting for transfers between devices, per_device(): lax.ppermute(theirs, 'groups', [(g, (g + 1) % groups) for g in range(grou...  2.42 us
    ppermute x1, starting transfers between devices, per_device(): lax.ppermute(theirs, 'groups', [(g, (g + 1) % groups) for g in range(grou...  1.49 us
  transfers between devices with their start and end apart: 6, of which 5 were waited for; matrix products, arithmetic and copies ran while one was open for 0% of the time, Pallas kernels for 12%

profile of v2, /device:TPU:0, one launch (start us, length us, event | category | flops | bytes accessed | tf_op | source)
XLA Modules:
  0.0 49.8 jit_solution(16423349239561446310)
XLA Ops:
  0.0 6.4 %all-gather = bf16[4,4,1792]{2,1,0:T(4,128)(2,1)S(1)} all-gather(bf16[1,4,1792]{2,1,0:T(4,128)(2,1)} %bitcast.13), channel_id=1, replica_groups=mesh['groups'=2,'gx'=8,'gy'=2] {'groups','gy'}, dimensions={0}, use_global_device_ids=true | all-gather | bytes 71680 | tf_op jit(solution)/shard_map/all_gather | solution.py:121
  6.4 11.4 %shard_map.37 = (f32[2,8,4608]{2,1,0:T(8,128)S(1)}, f32[2,8,4608]{2,1,0:T(8,128)S(1)}, bf16[16,1792]{1,0:T(8,128)(2,1)S(1)}) custom-call(bf16[16,1792]{1,0:T(8,128)(2,1)S(1)} %reshape.1.tokens_ref, bf16[1792,13312]{1,0:T(8,128)(2,1)} %gate_hbm.3, bf16[1792,13312]{1,0:T(8,128)(2,1)} %up_hbm.3), custom_call_target="tpu_custom_call" | custom-call | flops 528482304 | bytes 33030144 | tf_op jit(solution)/shard_map/pallas_call | solution.py:88
  17.8 2.1 %collective-permute-start = (f32[2,8,4608]{2,1,0:T(8,128)S(1)}, f32[2,8,4608]{2,1,0:T(8,128)S(1)}, u32[]{:S(2)}, u32[]{:S(2)}) collective-permute-start(f32[2,8,4608]{2,1,0:T(8,128)S(1)} %get-tuple-element.11), channel_id=1, source_target_pairs={{0,2},{1,5},{2,0},{3,7},{4,6},{5,1},{6,4},{7,3},{8,10},{9,13},{10,... | collective-permute-start | bytes 884744 | tf_op jit(solution)/shard_map/ppermute | solution.py:111
  19.9 6.1 %shard_map.38 = (f32[2,8,2048]{2,1,0:T(8,128)S(1)}, f32[2,8,2048]{2,1,0:T(8,128)S(1)}, bf16[16,1792]{1,0:T(8,128)(2,1)}) custom-call(bf16[16,1792]{1,0:T(8,128)(2,1)S(1)} %get-tuple-element.12.tokens_ref, bf16[1792,13312]{1,0:T(8,128)(2,1)} %gate_hbm.3, bf16[1792,13312]{1,0:T(8,128)(2,1)} %up_hbm.3), custom_call_target="tpu_custom_call" | custom-call | flops 234881024 | bytes 14680064 | tf_op jit(solution)/shard_map/pallas_call | solution.py:88
  26.0 0.1 collective-permute-start.2
  26.1 4.9 %collective-permute-done.2 = f32[2,8,2048]{2,1,0:T(8,128)S(1)} collective-permute-done((f32[2,8,2048]{2,1,0:T(8,128)S(1)}, f32[2,8,2048]{2,1,0:T(8,128)S(1)}, u32[]{:S(2)}, u32[]{:S(2)}) %collective-permute-start.2) | collective-permute-done | bytes 131104 | tf_op jit(solution)/shard_map/ppermute | solution.py:111
  31.1 1.6 %collective-permute-start.3 = (f32[2,4,2048]{2,1,0:T(4,128)S(1)}, f32[2,4,2048]{2,1,0:T(4,128)S(1)}, u32[]{:S(2)}, u32[]{:S(2)}) collective-permute-start(f32[2,4,2048]{2,1,0:T(4,128)S(1)} %slice.43), channel_id=1, source_target_pairs={{0,4},{1,3},{2,6},{3,1},{4,0},{5,7},{6,2},{7,5},{8,12},{9,11},{10,... | collective-permute-start | bytes 196616 | tf_op jit(solution)/shard_map/ppermute | solution.py:111
  32.7 0.0 collective-permute-done
  32.8 0.5 %collective-permute-start.1 = (f32[2,4,4608]{2,1,0:T(4,128)S(1)}, f32[2,4,4608]{2,1,0:T(4,128)S(1)}, u32[]{:S(2)}, u32[]{:S(2)}) collective-permute-start(f32[2,4,4608]{2,1,0:T(4,128)S(1)} %slice.41), channel_id=1, source_target_pairs={{0,4},{1,3},{2,6},{3,1},{4,0},{5,7},{6,2},{7,5},{8,12},{9,11},{10,... | collective-permute-start | bytes 442376 | tf_op jit(solution)/shard_map/ppermute | solution.py:111
  33.3 2.1 %collective-permute-done.3 = f32[2,4,2048]{2,1,0:T(4,128)S(1)} collective-permute-done((f32[2,4,2048]{2,1,0:T(4,128)S(1)}, f32[2,4,2048]{2,1,0:T(4,128)S(1)}, u32[]{:S(2)}, u32[]{:S(2)}) %collective-permute-start.3) | collective-permute-done | bytes 65568 | tf_op jit(solution)/shard_map/ppermute | solution.py:111
  35.4 2.6 %collective-permute-done.1 = f32[2,4,4608]{2,1,0:T(4,128)S(1)} collective-permute-done((f32[2,4,4608]{2,1,0:T(4,128)S(1)}, f32[2,4,4608]{2,1,0:T(4,128)S(1)}, u32[]{:S(2)}, u32[]{:S(2)}) %collective-permute-start.1) | collective-permute-done | bytes 147488 | tf_op jit(solution)/shard_map/ppermute | solution.py:111
  38.0 0.1 pad_maximum_fusion
  38.1 3.0 %collective-permute-start.4 = (f32[2,2,6656]{2,1,0:T(2,128)S(1)}, f32[2,2,6656]{2,1,0:T(2,128)S(1)}, u32[]{:S(2)}, u32[]{:S(2)}) collective-permute-start(f32[2,2,6656]{2,1,0:T(2,128)S(1)} %pad_maximum_fusion), channel_id=1, source_target_pairs={{0,8},{1,9},{2,10},{3,11},{4,12},{5,13},{6,14},{7,15},{8,0},{9,1},... | collective-permute-start | bytes 319496 | tf_op jit(solution)/shard_map/ppermute | solution.py:111
  41.2 3.8 %collective-permute-done.4 = f32[2,2,6656]{2,1,0:T(2,128)S(1)} collective-permute-done((f32[2,2,6656]{2,1,0:T(2,128)S(1)}, f32[2,2,6656]{2,1,0:T(2,128)S(1)}, u32[]{:S(2)}, u32[]{:S(2)}) %collective-permute-start.4) | collective-permute-done | bytes 106528 | tf_op jit(solution)/shard_map/ppermute | solution.py:111
  44.9 0.1 fusion.1
  45.0 0.1 fusion.3
  45.1 1.5 %collective-permute-start.5 = (bf16[1,6656]{1,0:T(2,128)(2,1)S(1)}, bf16[1,6656]{1,0:T(2,128)(2,1)S(1)}, u32[]{:S(2)}, u32[]{:S(2)}) collective-permute-start(bf16[1,6656]{1,0:T(2,128)(2,1)S(1)} %slice.49), channel_id=1, source_target_pairs={{0,16},{16,0},{1,17},{17,1},{2,18},{18,2},{3,19},{19,3},{4,20},{20... | collective-permute-start | bytes 39944 | tf_op jit(solution)/shard_map/ppermute | solution.py:140
  46.6 2.4 %collective-permute-done.5 = bf16[1,6656]{1,0:T(2,128)(2,1)S(1)} collective-permute-done((bf16[1,6656]{1,0:T(2,128)(2,1)S(1)}, bf16[1,6656]{1,0:T(2,128)(2,1)S(1)}, u32[]{:S(2)}, u32[]{:S(2)}) %collective-permute-start.5) | collective-permute-done | bytes 13344 | tf_op jit(solution)/shard_map/ppermute | solution.py:140
  49.0 0.1 broadcast_select_fusion.1
  49.1 0.7 %pad_maximum_fusion.1 = bf16[1,13312]{1,0:T(2,128)(2,1)} fusion(bf16[1,6656]{1,0:T(2,128)(2,1)S(1)} %get-tuple-element.16, bf16[1,6656]{1,0:T(2,128)(2,1)S(1)} %get-tuple-element.15), kind=kLoop, calls=%fused_computation.11 | loop fusion | flops 53248 | bytes 53248 | tf_op jit(solution)/shard_map/concatenate | solution.py:142
  (8 shorter events, 0.2 us)
Async XLA Ops:
  17.8 14.9 %collective-permute-start = (f32[2,8,4608]{2,1,0:T(8,128)S(1)}, f32[2,8,4608]{2,1,0:T(8,128)S(1)}, u32[]{:S(2)}, u32[]{:S(2)}) collective-permute-start(f32[2,8,4608]{2,1,0:T(8,128)S(1)} %get-tuple-element.11), channel_id=1, source_target_pairs={{0,2},{1,5},{2,0},{3,7},{4,6},{5,1},{6,4},{7,3},{8,10},{9,13},{10,... | collective-permute-start | bytes 884744 | tf_op jit(solution)/shard_map/ppermute | solution.py:111
  26.0 5.0 %collective-permute-start.2 = (f32[2,8,2048]{2,1,0:T(8,128)S(1)}, f32[2,8,2048]{2,1,0:T(8,128)S(1)}, u32[]{:S(2)}, u32[]{:S(2)}) collective-permute-start(f32[2,8,2048]{2,1,0:T(8,128)S(1)} %get-tuple-element.14), channel_id=1, source_target_pairs={{0,2},{1,5},{2,0},{3,7},{4,6},{5,1},{6,4},{7,3},{8,10},{9,13},{10,... | collective-permute-start | bytes 393224 | tf_op jit(solution)/shard_map/ppermute | solution.py:111
  31.1 4.3 %collective-permute-start.3 = (f32[2,4,2048]{2,1,0:T(4,128)S(1)}, f32[2,4,2048]{2,1,0:T(4,128)S(1)}, u32[]{:S(2)}, u32[]{:S(2)}) collective-permute-start(f32[2,4,2048]{2,1,0:T(4,128)S(1)} %slice.43), channel_id=1, source_target_pairs={{0,4},{1,3},{2,6},{3,1},{4,0},{5,7},{6,2},{7,5},{8,12},{9,11},{10,... | collective-permute-start | bytes 196616 | tf_op jit(solution)/shard_map/ppermute | solution.py:111
  32.8 5.2 %collective-permute-start.1 = (f32[2,4,4608]{2,1,0:T(4,128)S(1)}, f32[2,4,4608]{2,1,0:T(4,128)S(1)}, u32[]{:S(2)}, u32[]{:S(2)}) collective-permute-start(f32[2,4,4608]{2,1,0:T(4,128)S(1)} %slice.41), channel_id=1, source_target_pairs={{0,4},{1,3},{2,6},{3,1},{4,0},{5,7},{6,2},{7,5},{8,12},{9,11},{10,... | collective-permute-start | bytes 442376 | tf_op jit(solution)/shard_map/ppermute | solution.py:111
  38.1 6.8 %collective-permute-start.4 = (f32[2,2,6656]{2,1,0:T(2,128)S(1)}, f32[2,2,6656]{2,1,0:T(2,128)S(1)}, u32[]{:S(2)}, u32[]{:S(2)}) collective-permute-start(f32[2,2,6656]{2,1,0:T(2,128)S(1)} %pad_maximum_fusion), channel_id=1, source_target_pairs={{0,8},{1,9},{2,10},{3,11},{4,12},{5,13},{6,14},{7,15},{8,0},{9,1},... | collective-permute-start | bytes 319496 | tf_op jit(solution)/shard_map/ppermute | solution.py:111
  45.1 3.9 %collective-permute-start.5 = (bf16[1,6656]{1,0:T(2,128)(2,1)S(1)}, bf16[1,6656]{1,0:T(2,128)(2,1)S(1)}, u32[]{:S(2)}, u32[]{:S(2)}) collective-permute-start(bf16[1,6656]{1,0:T(2,128)(2,1)S(1)} %slice.49), channel_id=1, source_target_pairs={{0,16},{16,0},{1,17},{17,1},{2,18},{18,2},{3,19},{19,3},{4,20},{20... | collective-permute-start | bytes 39944 | tf_op jit(solution)/shard_map/ppermute | solution.py:140

commit v3 on v1

v3 whole, which is shorter than its diff:
```python
import functools

import jax
import jax.numpy as jnp
from jax import lax
from jax.experimental import pallas as pl
from jax.experimental.pallas import tpu as pltpu
from jax.sharding import PartitionSpec as P

LANES = 128


def masks(count, core):
    bits = [1 << b for b in range(count.bit_length() - 1)]
    if core % 2 and len(bits) > 1:
        bits[0], bits[1] = bits[1], bits[0]
    return bits


def column_block(width):
    units = width // LANES
    return LANES * max(d for d in range(1, min(units, 4) + 1) if units % d == 0)


def weight_copies(weights, target, sems, column, block):
    columns = pl.ds(pl.multiple_of(column * block, LANES), block)
    return [pltpu.make_async_copy(w.at[:, columns], target.at[i], sems.at[i]) for i, w in enumerate(weights)]


def fetch_kernel(all_blocks, block, gate_hbm, up_hbm, ahead_ref, sems):
    base = lax.axis_index("groups") * all_blocks
    copies = []
    for n in range(ahead_ref.shape[0]):
        copies += weight_copies((gate_hbm, up_hbm), ahead_ref.at[n], sems.at[n], base + n, block)
    for copy in copies:
        copy.start()
    for copy in copies:
        copy.wait()


def fetch(all_blocks, block, ahead, gate_weight, up_weight):
    depth = gate_weight.shape[0]
    return pl.pallas_call(
        functools.partial(fetch_kernel, all_blocks, block),
        in_specs=[pl.BlockSpec(memory_space=pl.ANY)] * 2,
        out_specs=pl.BlockSpec(memory_space=pltpu.VMEM),
        out_shape=jax.ShapeDtypeStruct((ahead, 2, depth, block), jnp.bfloat16),
        scratch_shapes=[pltpu.SemaphoreType.DMA((ahead, 2))],
        cost_estimate=pl.CostEstimate(flops=0, bytes_accessed=4 * depth * ahead * block, transcendentals=0),
        compiler_params=pltpu.CompilerParams(vmem_limit_bytes=16 << 20),
    )(gate_weight, up_weight)


def pick_rows(sizes, tokens):
    groups, gx, gy = sizes
    group, x, core = lax.axis_index("groups"), lax.axis_index("gx"), lax.axis_index("gy")
    rows = tokens.shape[0]
    each = rows // (groups * gx)
    held = rows // (groups * gy)
    m = lax.broadcasted_iota(jnp.int32, (rows, rows), 0)
    source = lax.broadcasted_iota(jnp.int32, (rows, rows), 1)
    j, q, i = m // (groups * each), (m // each) % groups, m % each
    mine, other = masks(gx, 0), masks(gx, 1)
    flip = jnp.zeros_like(j)
    for n in range(len(mine)):
        bit = (j // (1 << (len(mine) - 1 - n))) % 2
        flip = flip + bit * jnp.where(core == 0, mine[n], other[n])
    row = (x ^ flip) * each + i
    wanted = (q * gy + (row // held + gy - core) % gy) * held + row % held
    pick = (source == wanted).astype(jnp.bfloat16)
    return jnp.dot(pick, tokens, preferred_element_type=jnp.float32).astype(jnp.bfloat16)


def project_kernel(sizes, all_blocks, block, tokens_ref, ahead_ref, gate_hbm, up_hbm, send_ref, keep_ref, rows_ref, buffer, sems):
    base = lax.axis_index("groups") * all_blocks
    slots = buffer.shape[0]
    ahead = ahead_ref.shape[0]
    later = all_blocks - ahead

    def copies(i, slot):
        return weight_copies((gate_hbm, up_hbm), buffer.at[slot], sems.at[slot], base + ahead + i, block)

    for i in range(min(slots - 1, later)):
        for copy in copies(i, i):
            copy.start()

    rows_ref[...] = pick_rows(sizes, tokens_ref[...])
    half = rows_ref.shape[0] // 2

    def multiply(n, w, weights):
        columns = pl.ds(n * block if isinstance(n, int) else pl.multiple_of(n * block, LANES), block)
        total = jnp.dot(rows_ref[...], weights, preferred_element_type=jnp.float32)
        keep_ref[w, :, columns] = total[:half]
        send_ref[w, :, columns] = total[half:]

    for n in range(ahead):
        for w in range(2):
            multiply(n, w, ahead_ref[n, w])

    def step(n, carry):
        slot = lax.rem(n, slots)

        @pl.when(n + slots - 1 < later)
        def _():
            for copy in copies(n + slots - 1, lax.rem(n + slots - 1, slots)):
                copy.start()

        for w, copy in enumerate(copies(n, slot)):
            copy.wait()
            multiply(ahead + n, w, buffer[slot, w])
        return carry

    lax.fori_loop(0, later, step, 0)


def project(sizes, all_blocks, block, tokens, ahead, gate_weight, up_weight):
    rows, depth = tokens.shape
    width = all_blocks * block
    slots = 4
    shape = jax.ShapeDtypeStruct((2, rows // 2, width), jnp.float32)
    return pl.pallas_call(
        functools.partial(project_kernel, sizes, all_blocks, block),
        in_specs=[pl.BlockSpec(memory_space=pltpu.VMEM)] * 2 + [pl.BlockSpec(memory_space=pl.ANY)] * 2,
        out_specs=[pl.BlockSpec(memory_space=pltpu.VMEM)] * 2,
        out_shape=[shape, shape],
        scratch_shapes=[
            pltpu.VMEM((rows, depth), jnp.bfloat16),
            pltpu.VMEM((slots, 2, depth, block), jnp.bfloat16),
            pltpu.SemaphoreType.DMA((slots, 2)),
        ],
        cost_estimate=pl.CostEstimate(
            flops=4 * rows * depth * width, bytes_accessed=4 * depth * width, transcendentals=0
        ),
        compiler_params=pltpu.CompilerParams(vmem_limit_bytes=32 << 20),
    )(tokens, ahead, gate_weight, up_weight)


def gather_rows(sizes, tokens):
    groups, gx, gy = sizes
    both = [
        (g * gy + core, (g + 1) % groups * gy + (core + 1) % gy) for g in range(groups) for core in range(gy)
    ]
    across = lax.ppermute(tokens, "groups", [(g, (g + 1) % groups) for g in range(groups)])
    diagonal = lax.ppermute(tokens, ("groups", "gy"), both)
    beside = lax.ppermute(tokens, "gy", [(core, (core + 1) % gy) for core in range(gy)])
    return jnp.concatenate([tokens, beside, across, diagonal], axis=0)


def per_device(sizes, tokens, gate_weight, up_weight):
    groups, gx, gy = sizes
    width = gate_weight.shape[1] // groups
    block = column_block(width)
    all_blocks = width // block
    ahead = fetch(all_blocks, block, min(3, all_blocks), gate_weight, up_weight)
    rows = gather_rows(sizes, tokens)
    send, keep = project(sizes, all_blocks, block, rows, ahead, gate_weight, up_weight)
    phases = gx.bit_length() - 1
    for n in range(phases):
        pairs = [
            (x * gy + core, (x ^ masks(gx, core)[n]) * gy + core) for x in range(gx) for core in range(gy)
        ]
        total = keep + lax.ppermute(send, ("gx", "gy"), pairs)
        half = total.shape[1] // 2
        if n < phases - 1:
            keep, send = total[:, :half], total[:, half:]
    hidden = (jax.nn.silu(total[0]) * total[1]).astype(jnp.bfloat16)
    each = hidden.shape[0] // groups
    own, theirs = hidden[:each], hidden[each:]
    theirs = lax.ppermute(theirs, "groups", [(g, (g + 1) % groups) for g in range(groups)])
    first = lax.axis_index("groups") == 0
    return jnp.concatenate([jnp.where(first, own, theirs), jnp.where(first, theirs, own)], axis=1)


def solution(mesh):
    sizes = tuple(mesh.shape[name] for name in ("groups", "gx", "gy"))
    in_specs = (P(("groups", "gy"), "gx"), P("gx", "gy"), P("gx", "gy"))
    out_specs = P(("groups", "gx"), "gy")
    return jax.shard_map(
        functools.partial(per_device, sizes), mesh=mesh, in_specs=in_specs, out_specs=out_specs, check_vma=False
    )
```

time: 48.2 us -> 45.8 us (0.950)
  blocking collectives: 6.42 us -> 0 us
  starting transfers between devices: 10.1 us -> 12.4 us
  Pallas kernels: 15.7 us -> 16.8 us
  waiting for transfers between devices: 14.7 us -> 15.2 us
    all_gather x1 -> x0, blocking collectives: 6.42 us -> none  [per_device(): rows = lax.all_gather(tokens, ('groups', 'gy'), axis=0, tiled=True)]
    ppermute x0 -> x3, starting transfers between devices: none -> 3.09 us  [the longest x1 2.55 us: gather_rows(): lax.ppermute(tokens, 'groups', [(g, (g + 1) % groups) for g in range(grou...]
    pallas_call x1 -> x2, Pallas kernels: 15.7 us -> 16.8 us  [the longest x1 12.5 us: project(): pl.pallas_call(functools.partial(project_kernel, sizes, all_blocks, block...]
    ppermute x3, starting transfers between devices: 7.28 us -> 6.55 us  [per_device(): total = keep + lax.ppermute(send, ('gx', 'gy'), pairs)]
    ppermute x3, waiting for transfers between devices: 12.9 us -> 13.4 us  [per_device(): total = keep + lax.ppermute(send, ('gx', 'gy'), pairs)]
  transfers between devices with their start and end apart: 4 -> 7, of which waited for: 4 -> 4; matrix products, arithmetic and copies ran while one was open for 0% -> 0% of each run, Pallas kernels for 0% -> 9%
where the time goes in v3:
time: 45.8 us; the launch traced here: 45.7 us
  Pallas kernels  16.8 us (37%)
  waiting for transfers between devices  15.2 us (33%)
  starting transfers between devices  12.4 us (27%)
  other arithmetic  1.01 us (2%)
    ppermute x3, waiting for transfers between devices, per_device(): total = keep + lax.ppermute(send, ('gx', 'gy'), pairs)  13.4 us
    pallas_call x1, Pallas kernels, project(): pl.pallas_call(functools.partial(project_kernel, sizes, all_blocks, block...  12.5 us
    ppermute x3, starting transfers between devices, per_device(): total = keep + lax.ppermute(send, ('gx', 'gy'), pairs)  6.55 us
    pallas_call x1, Pallas kernels, fetch(): pl.pallas_call(functools.partial(fetch_kernel, all_blocks, block), in_spe...  4.32 us
    ppermute x1, starting transfers between devices, per_device(): lax.ppermute(theirs, 'groups', [(g, (g + 1) % groups) for g in range(grou...  2.78 us
    ppermute x1, starting transfers between devices, gather_rows(): lax.ppermute(tokens, 'groups', [(g, (g + 1) % groups) for g in range(grou...  2.55 us
    ppermute x1, waiting for transfers between devices, per_device(): lax.ppermute(theirs, 'groups', [(g, (g + 1) % groups) for g in range(grou...  1.83 us
  transfers between devices with their start and end apart: 7, of which 4 were waited for; matrix products, arithmetic and copies ran while one was open for 0% of the time, Pallas kernels for 9%

profile of v3, /device:TPU:0, one launch (start us, length us, event | category | flops | bytes accessed | tf_op | source)
XLA Modules:
  0.0 45.7 jit_solution(4222402706545356513)
XLA Ops:
  0.0 0.0 copy-start
  0.0 0.5 collective-permute-start
  0.5 2.5 %collective-permute-start.1 = (bf16[4,1792]{1,0:T(4,128)(2,1)}, bf16[4,1792]{1,0:T(4,128)(2,1)S(1)}, u32[]{:S(2)}, u32[]{:S(2)}) collective-permute-start(bf16[4,1792]{1,0:T(4,128)(2,1)} %param.3), channel_id=1, source_target_pairs={{0,16},{16,0},{1,17},{17,1},{2,18},{18,2},{3,19},{19,3},{4,20},{20... | collective-permute-start | bytes 43016 | tf_op jit(solution)/shard_map/ppermute | solution.py:143
  3.0 0.1 collective-permute-start.2
  3.1 4.3 %shard_map.37.ahead_ref = bf16[3,2,1792,512]{3,2,1,0:T(8,128)(2,1)S(1)} custom-call(bf16[1792,13312]{1,0:T(8,128)(2,1)} %gate_hbm.3, bf16[1792,13312]{1,0:T(8,128)(2,1)} %up_hbm.3), custom_call_target="tpu_custom_call" | custom-call | bytes 11010048 | tf_op jit(solution)/shard_map/pallas_call | solution.py:43
  7.4 0.0 collective-permute-done
  7.4 0.0 collective-permute-done.1
  7.4 0.0 collective-permute-done.2
  7.5 0.0 copy-done
  7.5 12.5 %shard_map.38 = (f32[2,8,6656]{2,1,0:T(8,128)S(1)}, f32[2,8,6656]{2,1,0:T(8,128)S(1)}) custom-call(bf16[16,1792]{1,0:T(8,128)(2,1)S(1)} %pad_maximum_fusion.tokens_ref, bf16[3,2,1792,512]{3,2,1,0:T(8,128)(2,1)S(1)} %shard_map.37.ahead_ref, bf16[1792,13312]{1,0:T(8,128)(2,1)} %gate_hbm.3, bf16[1792,13312]{1,0:T(8,128)(2,1)} %up_hbm.3), custom_call_target="tpu_custom_call" | custom-call | flops 763363328 | bytes 47710208 | tf_op jit(solution)/shard_map/pallas_call | solution.py:121
  20.0 1.8 %collective-permute-start.3 = (f32[2,8,6656]{2,1,0:T(8,128)S(1)}, f32[2,8,6656]{2,1,0:T(8,128)S(1)}, u32[]{:S(2)}, u32[]{:S(2)}) collective-permute-start(f32[2,8,6656]{2,1,0:T(8,128)S(1)} %get-tuple-element.8), channel_id=1, source_target_pairs={{0,2},{1,5},{2,0},{3,7},{4,6},{5,1},{6,4},{7,3},{8,10},{9,13},{10,... | collective-permute-start | bytes 1277960 | tf_op jit(solution)/shard_map/ppermute | solution.py:162
  21.8 6.4 %collective-permute-done.3 = f32[2,8,6656]{2,1,0:T(8,128)S(1)} collective-permute-done((f32[2,8,6656]{2,1,0:T(8,128)S(1)}, f32[2,8,6656]{2,1,0:T(8,128)S(1)}, u32[]{:S(2)}, u32[]{:S(2)}) %collective-permute-start.3) | collective-permute-done | bytes 426016 | tf_op jit(solution)/shard_map/ppermute | solution.py:162
  28.2 0.1 add.13
  28.3 1.9 %collective-permute-start.4 = (f32[2,4,6656]{2,1,0:T(4,128)S(1)}, f32[2,4,6656]{2,1,0:T(4,128)S(1)}, u32[]{:S(2)}, u32[]{:S(2)}) collective-permute-start(f32[2,4,6656]{2,1,0:T(4,128)S(1)} %slice.33), channel_id=1, source_target_pairs={{0,4},{1,3},{2,6},{3,1},{4,0},{5,7},{6,2},{7,5},{8,12},{9,11},{10,... | collective-permute-start | bytes 638984 | tf_op jit(solution)/shard_map/ppermute | solution.py:162
  30.2 4.0 %collective-permute-done.4 = f32[2,4,6656]{2,1,0:T(4,128)S(1)} collective-permute-done((f32[2,4,6656]{2,1,0:T(4,128)S(1)}, f32[2,4,6656]{2,1,0:T(4,128)S(1)}, u32[]{:S(2)}, u32[]{:S(2)}) %collective-permute-start.4) | collective-permute-done | bytes 213024 | tf_op jit(solution)/shard_map/ppermute | solution.py:162
  34.3 0.1 slice.35
  34.3 2.9 %collective-permute-start.5 = (f32[2,2,6656]{2,1,0:T(2,128)S(1)}, f32[2,2,6656]{2,1,0:T(2,128)S(1)}, u32[]{:S(2)}, u32[]{:S(2)}) collective-permute-start(f32[2,2,6656]{2,1,0:T(2,128)S(1)} %slice.35), channel_id=1, source_target_pairs={{0,8},{1,9},{2,10},{3,11},{4,12},{5,13},{6,14},{7,15},{8,0},{9,1},... | collective-permute-start | bytes 319496 | tf_op jit(solution)/shard_map/ppermute | solution.py:162
  37.2 2.9 %collective-permute-done.5 = f32[2,2,6656]{2,1,0:T(2,128)S(1)} collective-permute-done((f32[2,2,6656]{2,1,0:T(2,128)S(1)}, f32[2,2,6656]{2,1,0:T(2,128)S(1)}, u32[]{:S(2)}, u32[]{:S(2)}) %collective-permute-start.5) | collective-permute-done | bytes 106528 | tf_op jit(solution)/shard_map/ppermute | solution.py:162
  40.1 0.1 slice_add_fusion.1
  40.2 0.1 fusion.1
  40.3 2.8 %collective-permute-start.6 = (bf16[1,6656]{1,0:T(2,128)(2,1)S(1)}, bf16[1,6656]{1,0:T(2,128)(2,1)S(1)}, u32[]{:S(2)}, u32[]{:S(2)}) collective-permute-start(bf16[1,6656]{1,0:T(2,128)(2,1)S(1)} %slice.39), channel_id=1, source_target_pairs={{0,16},{16,0},{1,17},{17,1},{2,18},{18,2},{3,19},{19,3},{4,20},{20... | collective-permute-start | bytes 39944 | tf_op jit(solution)/shard_map/ppermute | solution.py:169
  43.1 1.8 %collective-permute-done.6 = bf16[1,6656]{1,0:T(2,128)(2,1)S(1)} collective-permute-done((bf16[1,6656]{1,0:T(2,128)(2,1)S(1)}, bf16[1,6656]{1,0:T(2,128)(2,1)S(1)}, u32[]{:S(2)}, u32[]{:S(2)}) %collective-permute-start.6) | collective-permute-done | bytes 13344 | tf_op jit(solution)/shard_map/ppermute | solution.py:169
  44.9 0.1 broadcast_select_fusion.1
  45.0 0.7 %pad_maximum_fusion.1 = bf16[1,13312]{1,0:T(2,128)(2,1)} fusion(bf16[1,6656]{1,0:T(2,128)(2,1)S(1)} %get-tuple-element.10, bf16[1,6656]{1,0:T(2,128)(2,1)S(1)} %get-tuple-element.9), kind=kLoop, calls=%fused_computation.7 | loop fusion | flops 53248 | bytes 53248 | tf_op jit(solution)/shard_map/concatenate | solution.py:171
  (4 shorter events, 0.2 us)
Async XLA Ops:
  0.0 7.5 %copy-start = (bf16[4,1792]{1,0:T(4,128)(2,1)S(1)}, bf16[4,1792]{1,0:T(4,128)(2,1)}, u32[]{:S(2)}) copy-start(bf16[4,1792]{1,0:T(4,128)(2,1)} %param.3) | copy-start | bytes 43012
  0.0 7.4 %collective-permute-start = (bf16[4,1792]{1,0:T(4,128)(2,1)}, bf16[4,1792]{1,0:T(4,128)(2,1)S(1)}, u32[]{:S(2)}, u32[]{:S(2)}) collective-permute-start(bf16[4,1792]{1,0:T(4,128)(2,1)} %param.3), channel_id=1, source_target_pairs={{0,1},{1,0},{2,3},{3,2},{4,5},{5,4},{6,7},{7,6},{8,9},{9,8},{10,11... | collective-permute-start | bytes 43016 | tf_op jit(solution)/shard_map/ppermute | solution.py:145
  0.5 7.0 %collective-permute-start.1 = (bf16[4,1792]{1,0:T(4,128)(2,1)}, bf16[4,1792]{1,0:T(4,128)(2,1)S(1)}, u32[]{:S(2)}, u32[]{:S(2)}) collective-permute-start(bf16[4,1792]{1,0:T(4,128)(2,1)} %param.3), channel_id=1, source_target_pairs={{0,16},{16,0},{1,17},{17,1},{2,18},{18,2},{3,19},{19,3},{4,20},{20... | collective-permute-start | bytes 43016 | tf_op jit(solution)/shard_map/ppermute | solution.py:143
  3.0 4.4 %collective-permute-start.2 = (bf16[4,1792]{1,0:T(4,128)(2,1)}, bf16[4,1792]{1,0:T(4,128)(2,1)S(1)}, u32[]{:S(2)}, u32[]{:S(2)}) collective-permute-start(bf16[4,1792]{1,0:T(4,128)(2,1)} %param.3), channel_id=1, source_target_pairs={{0,17},{1,16},{16,1},{17,0},{2,19},{3,18},{18,3},{19,2},{4,21},{5,... | collective-permute-start | bytes 43016 | tf_op jit(solution)/shard_map/ppermute | solution.py:144
  20.0 8.2 %collective-permute-start.3 = (f32[2,8,6656]{2,1,0:T(8,128)S(1)}, f32[2,8,6656]{2,1,0:T(8,128)S(1)}, u32[]{:S(2)}, u32[]{:S(2)}) collective-permute-start(f32[2,8,6656]{2,1,0:T(8,128)S(1)} %get-tuple-element.8), channel_id=1, source_target_pairs={{0,2},{1,5},{2,0},{3,7},{4,6},{5,1},{6,4},{7,3},{8,10},{9,13},{10,... | collective-permute-start | bytes 1277960 | tf_op jit(solution)/shard_map/ppermute | solution.py:162
  28.3 5.9 %collective-permute-start.4 = (f32[2,4,6656]{2,1,0:T(4,128)S(1)}, f32[2,4,6656]{2,1,0:T(4,128)S(1)}, u32[]{:S(2)}, u32[]{:S(2)}) collective-permute-start(f32[2,4,6656]{2,1,0:T(4,128)S(1)} %slice.33), channel_id=1, source_target_pairs={{0,4},{1,3},{2,6},{3,1},{4,0},{5,7},{6,2},{7,5},{8,12},{9,11},{10,... | collective-permute-start | bytes 638984 | tf_op jit(solution)/shard_map/ppermute | solution.py:162
  34.3 5.8 %collective-permute-start.5 = (f32[2,2,6656]{2,1,0:T(2,128)S(1)}, f32[2,2,6656]{2,1,0:T(2,128)S(1)}, u32[]{:S(2)}, u32[]{:S(2)}) collective-permute-start(f32[2,2,6656]{2,1,0:T(2,128)S(1)} %slice.35), channel_id=1, source_target_pairs={{0,8},{1,9},{2,10},{3,11},{4,12},{5,13},{6,14},{7,15},{8,0},{9,1},... | collective-permute-start | bytes 319496 | tf_op jit(solution)/shard_map/ppermute | solution.py:162
  40.3 4.6 %collective-permute-start.6 = (bf16[1,6656]{1,0:T(2,128)(2,1)S(1)}, bf16[1,6656]{1,0:T(2,128)(2,1)S(1)}, u32[]{:S(2)}, u32[]{:S(2)}) collective-permute-start(bf16[1,6656]{1,0:T(2,128)(2,1)S(1)} %slice.39), channel_id=1, source_target_pairs={{0,16},{16,0},{1,17},{17,1},{2,18},{18,2},{3,19},{19,3},{4,20},{20... | collective-permute-start | bytes 39944 | tf_op jit(solution)/shard_map/ppermute | solution.py:169

commit v4 on v3

--- a/solution.py
+++ b/solution.py
@@ -8,6 +8,27 @@
 from jax.sharding import PartitionSpec as P
 
 LANES = 128
+POWER = 64
+FLOOR = 2.0 ** (-120.0 / POWER)
+SCALE = 2.0 ** (120.0 / POWER) - FLOOR
+LEAST = 2.0**-100
+
+
+def encode(y, bound):
+    code = jnp.abs(y) * (SCALE / bound) + FLOOR
+    for _ in range(POWER.bit_length() - 1):
+        code = code * code
+    return jnp.where(y < 0, -code, code).astype(jnp.bfloat16)
+
+
+def decode(code, bound):
+    code = code.astype(jnp.float32)
+    y = (jnp.exp(jnp.log(jnp.abs(code)) * (1.0 / POWER)) - FLOOR) * (bound * (1.0 / SCALE))
+    return jnp.where(code < 0, -y, y)
+
+
+def rounded_up(bound):
+    return lax.reduce_precision(jnp.maximum(bound * (1.0 + 2.0**-6), LEAST), 8, 7)
 
 
 def masks(count, core):
@@ -71,7 +92,7 @@
     return jnp.dot(pick, tokens, preferred_element_type=jnp.float32).astype(jnp.bfloat16)
 
 
-def project_kernel(sizes, all_blocks, block, tokens_ref, ahead_ref, gate_hbm, up_hbm, send_ref, keep_ref, rows_ref, buffer, sems):
+def project_kernel(sizes, all_blocks, block, tokens_ref, ahead_ref, gate_hbm, up_hbm, send_ref, keep_ref, rows_ref, half_ref, buffer, sems):
     base = lax.axis_index("groups") * all_blocks
     slots = buffer.shape[0]
     ahead = ahead_ref.shape[0]
@@ -87,11 +108,14 @@
     rows_ref[...] = pick_rows(sizes, tokens_ref[...])
     half = rows_ref.shape[0] // 2
 
+    tiles = block // LANES
+
     def multiply(n, w, weights):
-        columns = pl.ds(n * block if isinstance(n, int) else pl.multiple_of(n * block, LANES), block)
         total = jnp.dot(rows_ref[...], weights, preferred_element_type=jnp.float32)
-        keep_ref[w, :, columns] = total[:half]
-        send_ref[w, :, columns] = total[half:]
+        for t in range(tiles):
+            tile = total[:, t * LANES : (t + 1) * LANES]
+            keep_ref[w, n * tiles + t] = tile[:half]
+            half_ref[w, n * tiles + t] = tile[half:]
 
     for n in range(ahead):
         for w in range(2):
@@ -112,19 +136,40 @@
 
     lax.fori_loop(0, later, step, 0)
 
+    every = all_blocks * tiles
+    def bound_of(ref, w):
+        peak = jnp.zeros((half, LANES), jnp.float32)
+        for n in range(all_blocks):
+            peak = jnp.maximum(peak, jnp.max(jnp.abs(ref[w, n * tiles : (n + 1) * tiles]), axis=0))
+        peak = jnp.broadcast_to(jnp.max(peak, axis=1, keepdims=True), (half, LANES))
+        return jnp.maximum(peak * (1.0 + 2.0**-6), LEAST).astype(jnp.bfloat16)
+
+    for w in range(2):
+        keep_ref[w, every] = bound_of(keep_ref, w).astype(jnp.float32)
+        bound = bound_of(half_ref, w)
+        send_ref[w, every] = bound
+        bound = bound.astype(jnp.float32)
+        for n in range(all_blocks):
+            now = slice(n * tiles, (n + 1) * tiles)
+            send_ref[w, now] = encode(half_ref[w, now], bound[None])
+
 
 def project(sizes, all_blocks, block, tokens, ahead, gate_weight, up_weight):
     rows, depth = tokens.shape
     width = all_blocks * block
     slots = 4
-    shape = jax.ShapeDtypeStruct((2, rows // 2, width), jnp.float32)
+    half = rows // 2
     return pl.pallas_call(
         functools.partial(project_kernel, sizes, all_blocks, block),
         in_specs=[pl.BlockSpec(memory_space=pltpu.VMEM)] * 2 + [pl.BlockSpec(memory_space=pl.ANY)] * 2,
         out_specs=[pl.BlockSpec(memory_space=pltpu.VMEM)] * 2,
-        out_shape=[shape, shape],
+        out_shape=[
+            jax.ShapeDtypeStruct((2, width // LANES + 1, half, LANES), jnp.bfloat16),
+            jax.ShapeDtypeStruct((2, width // LANES + 1, half, LANES), jnp.float32),
+        ],
         scratch_shapes=[
             pltpu.VMEM((rows, depth), jnp.bfloat16),
+            pltpu.VMEM((2, width // LANES, half, LANES), jnp.float32),
             pltpu.VMEM((slots, 2, depth, block), jnp.bfloat16),
             pltpu.SemaphoreType.DMA((slots, 2)),
         ],
@@ -154,16 +199,23 @@
     ahead = fetch(all_blocks, block, min(3, all_blocks), gate_weight, up_weight)
     rows = gather_rows(sizes, tokens)
     send, keep = project(sizes, all_blocks, block, rows, ahead, gate_weight, up_weight)
+    keep, bound = keep[:, :-1], keep[:, -1:]
     phases = gx.bit_length() - 1
     for n in range(phases):
         pairs = [
             (x * gy + core, (x ^ masks(gx, core)[n]) * gy + core) for x in range(gx) for core in range(gy)
         ]
-        total = keep + lax.ppermute(send, ("gx", "gy"), pairs)
-        half = total.shape[1] // 2
+        came = lax.ppermute(send, ("gx", "gy"), pairs)
+        came, came_bound = came[:, :-1], came[:, -1:].astype(jnp.float32)
+        total = keep + decode(came, came_bound)
+        half = total.shape[2] // 2
         if n < phases - 1:
-            keep, send = total[:, :half], total[:, half:]
+            bound = rounded_up(bound + came_bound)
+            send = encode(total[:, :, half:], bound[:, :, half:])
+            send = jnp.concatenate([send, bound[:, :, half:].astype(jnp.bfloat16)], axis=1)
+            keep, bound = total[:, :, :half], bound[:, :, :half]
     hidden = (jax.nn.silu(total[0]) * total[1]).astype(jnp.bfloat16)
+    hidden = jnp.swapaxes(hidden, 0, 1).reshape(hidden.shape[1], width)
     each = hidden.shape[0] // groups
     own, theirs = hidden[:each], hidden[each:]
     theirs = lax.ppermute(theirs, "groups", [(g, (g + 1) % groups) for g in range(groups)])

time: 45.8 us -> 42.3 us (0.924)
  waiting for transfers between devices: 15.2 us -> 11.5 us
  other arithmetic: 1.01 us -> 2.05 us
  starting transfers between devices: 12.4 us -> 11.4 us
    ppermute x3, waiting for transfers between devices: 13.4 us -> 9.31 us  [per_device(): came = lax.ppermute(send, ('gx', 'gy'), pairs)]
    ppermute x1, starting transfers between devices: 2.78 us -> 1.77 us  [per_device(): lax.ppermute(theirs, 'groups', [(g, (g + 1) % groups) for g in range(grou...]
  transfers between devices with their start and end apart: 7 -> 7, of which waited for: 4 -> 4; matrix products, arithmetic and copies ran while one was open for 0% -> 0% of each run, Pallas kernels for 9% -> 10%
where the time goes in v4:
time: 42.3 us; the launch traced here: 42.2 us
  Pallas kernels  17.1 us (40%)
  waiting for transfers between devices  11.5 us (27%)
  starting transfers between devices  11.4 us (27%)
  other arithmetic  2.05 us (5%)
    pallas_call x1, Pallas kernels, project(): pl.pallas_call(functools.partial(project_kernel, sizes, all_blocks, block...  12.8 us
    ppermute x3, waiting for transfers between devices, per_device(): came = lax.ppermute(send, ('gx', 'gy'), pairs)  9.31 us
    ppermute x3, starting transfers between devices, per_device(): came = lax.ppermute(send, ('gx', 'gy'), pairs)  6.55 us
    pallas_call x1, Pallas kernels, fetch(): pl.pallas_call(functools.partial(fetch_kernel, all_blocks, block), in_spe...  4.32 us
    ppermute x1, starting transfers between devices, gather_rows(): lax.ppermute(tokens, 'groups', [(g, (g + 1) % groups) for g in range(grou...  2.55 us
    ppermute x1, waiting for transfers between devices, per_device(): lax.ppermute(theirs, 'groups', [(g, (g + 1) % groups) for g in range(grou...  2.15 us
    ppermute x1, starting transfers between devices, per_device(): lax.ppermute(theirs, 'groups', [(g, (g + 1) % groups) for g in range(grou...  1.77 us
  transfers between devices with their start and end apart: 7, of which 4 were waited for; matrix products, arithmetic and copies ran while one was open for 0% of the time, Pallas kernels for 10%

profile of v4, /device:TPU:0, one launch (start us, length us, event | category | flops | bytes accessed | tf_op | source)
XLA Modules:
  0.0 42.2 jit_solution(1855381166793872837)
XLA Ops:
  0.0 0.0 copy-start
  0.0 0.5 %collective-permute-start = (bf16[4,1792]{1,0:T(4,128)(2,1)}, bf16[4,1792]{1,0:T(4,128)(2,1)S(1)}, u32[]{:S(2)}, u32[]{:S(2)}) collective-permute-start(bf16[4,1792]{1,0:T(4,128)(2,1)} %param.3), channel_id=1, source_target_pairs={{0,1},{1,0},{2,3},{3,2},{4,5},{5,4},{6,7},{7,6},{8,9},{9,8},{10,11... | collective-permute-start | bytes 43016 | tf_op jit(solution)/shard_map/ppermute | solution.py:190
  0.5 2.5 %collective-permute-start.1 = (bf16[4,1792]{1,0:T(4,128)(2,1)}, bf16[4,1792]{1,0:T(4,128)(2,1)S(1)}, u32[]{:S(2)}, u32[]{:S(2)}) collective-permute-start(bf16[4,1792]{1,0:T(4,128)(2,1)} %param.3), channel_id=1, source_target_pairs={{0,16},{16,0},{1,17},{17,1},{2,18},{18,2},{3,19},{19,3},{4,20},{20... | collective-permute-start | bytes 43016 | tf_op jit(solution)/shard_map/ppermute | solution.py:188
  3.0 0.1 collective-permute-start.2
  3.1 4.3 %shard_map.37.ahead_ref = bf16[3,2,1792,512]{3,2,1,0:T(8,128)(2,1)S(1)} custom-call(bf16[1792,13312]{1,0:T(8,128)(2,1)} %gate_hbm.3, bf16[1792,13312]{1,0:T(8,128)(2,1)} %up_hbm.3), custom_call_target="tpu_custom_call" | custom-call | bytes 11010048 | tf_op jit(solution)/shard_map/pallas_call | solution.py:64
  7.4 0.0 collective-permute-done
  7.4 0.0 collective-permute-done.1
  7.4 0.0 collective-permute-done.2
  7.5 0.0 copy-done
  7.5 12.8 %shard_map.38 = (bf16[2,53,8,128]{3,2,1,0:T(8,128)(2,1)S(1)}, f32[2,53,8,128]{3,2,1,0:T(8,128)S(1)}) custom-call(bf16[16,1792]{1,0:T(8,128)(2,1)S(1)} %pad_maximum_fusion.1.tokens_ref, bf16[3,2,1792,512]{3,2,1,0:T(8,128)(2,1)S(1)} %shard_map.37.ahead_ref, bf16[1792,13312]{1,0:T(8,128)(2,1)} %gate_hbm.3, bf16[1792,13312]{1,0:T(8,128)(2,1)} %up_hbm.3), custom_call_target="tpu_custom_call" | custom-call | flops 763363328 | bytes 47710208 | tf_op jit(solution)/shard_map/pallas_call | solution.py:162
  20.3 1.8 %collective-permute-start.3 = (bf16[2,53,8,128]{3,2,1,0:T(8,128)(2,1)S(1)}, bf16[2,53,8,128]{3,2,1,0:T(8,128)(2,1)S(1)}, u32[]{:S(2)}, u32[]{:S(2)}) collective-permute-start(bf16[2,53,8,128]{3,2,1,0:T(8,128)(2,1)S(1)} %get-tuple-element.8), channel_id=1, source_target_pairs={{0,2},{1,5},{2,0},{3,7},{4,6},{5,1},{6,4},{7,3},{8,10},{9,13},{10,... | collective-permute-start | bytes 651272 | tf_op jit(solution)/shard_map/ppermute | solution.py:208
  22.1 4.1 %collective-permute-done.3 = bf16[2,53,8,128]{3,2,1,0:T(8,128)(2,1)S(1)} collective-permute-done((bf16[2,53,8,128]{3,2,1,0:T(8,128)(2,1)S(1)}, bf16[2,53,8,128]{3,2,1,0:T(8,128)(2,1)S(1)}, u32[]{:S(2)}, u32[]{:S(2)}) %collective-permute-start.3) | collective-permute-done | bytes 217120 | tf_op jit(solution)/shard_map/ppermute | solution.py:208
  26.3 0.2 fusion.5
  26.5 0.2 fusion.12
  26.7 0.1 pad_maximum_fusion
  26.8 1.9 %collective-permute-start.4 = (bf16[2,53,4,128]{3,2,1,0:T(4,128)(2,1)S(1)}, bf16[2,53,4,128]{3,2,1,0:T(4,128)(2,1)S(1)}, u32[]{:S(2)}, u32[]{:S(2)}) collective-permute-start(bf16[2,53,4,128]{3,2,1,0:T(4,128)(2,1)S(1)} %pad_maximum_fusion), channel_id=1, source_target_pairs={{0,4},{1,3},{2,6},{3,1},{4,0},{5,7},{6,2},{7,5},{8,12},{9,11},{10,... | collective-permute-start | bytes 325640 | tf_op jit(solution)/shard_map/ppermute | solution.py:208
  28.6 2.9 %collective-permute-done.4 = bf16[2,53,4,128]{3,2,1,0:T(4,128)(2,1)S(1)} collective-permute-done((bf16[2,53,4,128]{3,2,1,0:T(4,128)(2,1)S(1)}, bf16[2,53,4,128]{3,2,1,0:T(4,128)(2,1)S(1)}, u32[]{:S(2)}, u32[]{:S(2)}) %collective-permute-start.4) | collective-permute-done | bytes 108576 | tf_op jit(solution)/shard_map/ppermute | solution.py:208
  31.6 0.2 fusion.11
  31.8 0.2 fusion.19
  32.0 0.1 pad_maximum_fusion.2
  32.1 2.9 %collective-permute-start.5 = (bf16[2,53,2,128]{3,2,1,0:T(2,128)(2,1)S(1)}, bf16[2,53,2,128]{3,2,1,0:T(2,128)(2,1)S(1)}, u32[]{:S(2)}, u32[]{:S(2)}) collective-permute-start(bf16[2,53,2,128]{3,2,1,0:T(2,128)(2,1)S(1)} %pad_maximum_fusion.2), channel_id=1, source_target_pairs={{0,8},{1,9},{2,10},{3,11},{4,12},{5,13},{6,14},{7,15},{8,0},{9,1},... | collective-permute-start | bytes 162824 | tf_op jit(solution)/shard_map/ppermute | solution.py:208
  35.0 2.2 %collective-permute-done.5 = bf16[2,53,2,128]{3,2,1,0:T(2,128)(2,1)S(1)} collective-permute-done((bf16[2,53,2,128]{3,2,1,0:T(2,128)(2,1)S(1)}, bf16[2,53,2,128]{3,2,1,0:T(2,128)(2,1)S(1)}, u32[]{:S(2)}, u32[]{:S(2)}) %collective-permute-start.5) | collective-permute-done | bytes 54304 | tf_op jit(solution)/shard_map/ppermute | solution.py:208
  37.2 0.2 fusion.18
  37.4 0.1 fusion.22
  37.5 1.8 %collective-permute-start.6 = (bf16[1,6656]{1,0:T(2,128)(2,1)S(1)}, bf16[1,6656]{1,0:T(2,128)(2,1)S(1)}, u32[]{:S(2)}, u32[]{:S(2)}) collective-permute-start(bf16[1,6656]{1,0:T(2,128)(2,1)S(1)} %slice_bitcast_fusion.2), channel_id=1, source_target_pairs={{0,16},{16,0},{1,17},{17,1},{2,18},{18,2},{3,19},{19,3},{4,20},{20... | collective-permute-start | bytes 39944 | tf_op jit(solution)/shard_map/ppermute | solution.py:221
  39.3 2.1 %collective-permute-done.6 = bf16[1,6656]{1,0:T(2,128)(2,1)S(1)} collective-permute-done((bf16[1,6656]{1,0:T(2,128)(2,1)S(1)}, bf16[1,6656]{1,0:T(2,128)(2,1)S(1)}, u32[]{:S(2)}, u32[]{:S(2)}) %collective-permute-start.6) | collective-permute-done | bytes 13344 | tf_op jit(solution)/shard_map/ppermute | solution.py:221
  41.5 0.1 broadcast_select_fusion.1
  41.5 0.7 %pad_maximum_fusion.3 = bf16[1,13312]{1,0:T(2,128)(2,1)} fusion(bf16[1,6656]{1,0:T(2,128)(2,1)S(1)} %get-tuple-element.14, bf16[1,6656]{1,0:T(2,128)(2,1)S(1)} %get-tuple-element.13), kind=kLoop, calls=%fused_computation.37 | loop fusion | flops 53248 | bytes 53248 | tf_op jit(solution)/shard_map/concatenate | solution.py:223
  (9 shorter events, 0.1 us)
Async XLA Ops:
  0.0 7.5 %copy-start = (bf16[4,1792]{1,0:T(4,128)(2,1)S(1)}, bf16[4,1792]{1,0:T(4,128)(2,1)}, u32[]{:S(2)}) copy-start(bf16[4,1792]{1,0:T(4,128)(2,1)} %param.3) | copy-start | bytes 43012
  0.0 7.4 %collective-permute-start = (bf16[4,1792]{1,0:T(4,128)(2,1)}, bf16[4,1792]{1,0:T(4,128)(2,1)S(1)}, u32[]{:S(2)}, u32[]{:S(2)}) collective-permute-start(bf16[4,1792]{1,0:T(4,128)(2,1)} %param.3), channel_id=1, source_target_pairs={{0,1},{1,0},{2,3},{3,2},{4,5},{5,4},{6,7},{7,6},{8,9},{9,8},{10,11... | collective-permute-start | bytes 43016 | tf_op jit(solution)/shard_map/ppermute | solution.py:190
  0.5 7.0 %collective-permute-start.1 = (bf16[4,1792]{1,0:T(4,128)(2,1)}, bf16[4,1792]{1,0:T(4,128)(2,1)S(1)}, u32[]{:S(2)}, u32[]{:S(2)}) collective-permute-start(bf16[4,1792]{1,0:T(4,128)(2,1)} %param.3), channel_id=1, source_target_pairs={{0,16},{16,0},{1,17},{17,1},{2,18},{18,2},{3,19},{19,3},{4,20},{20... | collective-permute-start | bytes 43016 | tf_op jit(solution)/shard_map/ppermute | solution.py:188
  3.0 4.4 %collective-permute-start.2 = (bf16[4,1792]{1,0:T(4,128)(2,1)}, bf16[4,1792]{1,0:T(4,128)(2,1)S(1)}, u32[]{:S(2)}, u32[]{:S(2)}) collective-permute-start(bf16[4,1792]{1,0:T(4,128)(2,1)} %param.3), channel_id=1, source_target_pairs={{0,17},{1,16},{16,1},{17,0},{2,19},{3,18},{18,3},{19,2},{4,21},{5,... | collective-permute-start | bytes 43016 | tf_op jit(solution)/shard_map/ppermute | solution.py:189
  20.3 6.0 %collective-permute-start.3 = (bf16[2,53,8,128]{3,2,1,0:T(8,128)(2,1)S(1)}, bf16[2,53,8,128]{3,2,1,0:T(8,128)(2,1)S(1)}, u32[]{:S(2)}, u32[]{:S(2)}) collective-permute-start(bf16[2,53,8,128]{3,2,1,0:T(8,128)(2,1)S(1)} %get-tuple-element.8), channel_id=1, source_target_pairs={{0,2},{1,5},{2,0},{3,7},{4,6},{5,1},{6,4},{7,3},{8,10},{9,13},{10,... | collective-permute-start | bytes 651272 | tf_op jit(solution)/shard_map/ppermute | solution.py:208
  26.8 4.8 %collective-permute-start.4 = (bf16[2,53,4,128]{3,2,1,0:T(4,128)(2,1)S(1)}, bf16[2,53,4,128]{3,2,1,0:T(4,128)(2,1)S(1)}, u32[]{:S(2)}, u32[]{:S(2)}) collective-permute-start(bf16[2,53,4,128]{3,2,1,0:T(4,128)(2,1)S(1)} %pad_maximum_fusion), channel_id=1, source_target_pairs={{0,4},{1,3},{2,6},{3,1},{4,0},{5,7},{6,2},{7,5},{8,12},{9,11},{10,... | collective-permute-start | bytes 325640 | tf_op jit(solution)/shard_map/ppermute | solution.py:208
  32.1 5.1 %collective-permute-start.5 = (bf16[2,53,2,128]{3,2,1,0:T(2,128)(2,1)S(1)}, bf16[2,53,2,128]{3,2,1,0:T(2,128)(2,1)S(1)}, u32[]{:S(2)}, u32[]{:S(2)}) collective-permute-start(bf16[2,53,2,128]{3,2,1,0:T(2,128)(2,1)S(1)} %pad_maximum_fusion.2), channel_id=1, source_target_pairs={{0,8},{1,9},{2,10},{3,11},{4,12},{5,13},{6,14},{7,15},{8,0},{9,1},... | collective-permute-start | bytes 162824 | tf_op jit(solution)/shard_map/ppermute | solution.py:208
  37.5 3.9 %collective-permute-start.6 = (bf16[1,6656]{1,0:T(2,128)(2,1)S(1)}, bf16[1,6656]{1,0:T(2,128)(2,1)S(1)}, u32[]{:S(2)}, u32[]{:S(2)}) collective-permute-start(bf16[1,6656]{1,0:T(2,128)(2,1)S(1)} %slice_bitcast_fusion.2), channel_id=1, source_target_pairs={{0,16},{16,0},{1,17},{17,1},{2,18},{18,2},{3,19},{19,3},{4,20},{20... | collective-permute-start | bytes 39944 | tf_op jit(solution)/shard_map/ppermute | solution.py:221

commit v5 on v3

--- a/solution.py
+++ b/solution.py
@@ -8,6 +8,27 @@
 from jax.sharding import PartitionSpec as P
 
 LANES = 128
+POWER = 64
+FLOOR = 2.0 ** (-120.0 / POWER)
+SCALE = 2.0 ** (120.0 / POWER) - FLOOR
+LEAST = 2.0**-100
+
+
+def encode(y, bound):
+    code = jnp.abs(y) * (SCALE / bound) + FLOOR
+    for _ in range(POWER.bit_length() - 1):
+        code = code * code
+    return jnp.where(y < 0, -code, code).astype(jnp.bfloat16)
+
+
+def decode(code, bound):
+    code = code.astype(jnp.float32)
+    y = (jnp.exp(jnp.log(jnp.abs(code)) * (1.0 / POWER)) - FLOOR) * (bound * (1.0 / SCALE))
+    return jnp.where(code < 0, -y, y)
+
+
+def rounded_up(bound):
+    return lax.reduce_precision(jnp.maximum(bound * (1.0 + 2.0**-6), LEAST), 8, 7)
 
 
 def masks(count, core):
@@ -51,14 +72,16 @@
     )(gate_weight, up_weight)
 
 
-def pick_rows(sizes, tokens):
+def pick_rows(sizes, tokens, w):
     groups, gx, gy = sizes
     group, x, core = lax.axis_index("groups"), lax.axis_index("gx"), lax.axis_index("gy")
     rows = tokens.shape[0]
     each = rows // (groups * gx)
     held = rows // (groups * gy)
-    m = lax.broadcasted_iota(jnp.int32, (rows, rows), 0)
+    quarter = rows // 4
+    place = lax.broadcasted_iota(jnp.int32, (rows, rows), 0)
     source = lax.broadcasted_iota(jnp.int32, (rows, rows), 1)
+    m = (place // quarter ^ w) * quarter + place % quarter
     j, q, i = m // (groups * each), (m // each) % groups, m % each
     mine, other = masks(gx, 0), masks(gx, 1)
     flip = jnp.zeros_like(j)
@@ -71,7 +94,10 @@
     return jnp.dot(pick, tokens, preferred_element_type=jnp.float32).astype(jnp.bfloat16)
 
 
-def project_kernel(sizes, all_blocks, block, tokens_ref, ahead_ref, gate_hbm, up_hbm, send_ref, keep_ref, rows_ref, buffer, sems):
+def project_kernel(
+    sizes, all_blocks, block, tokens_ref, ahead_ref, gate_hbm, up_hbm, keep_ref, *refs
+):
+    *send_refs, rows_ref, total_ref, buffer, sems = refs
     base = lax.axis_index("groups") * all_blocks
     slots = buffer.shape[0]
     ahead = ahead_ref.shape[0]
@@ -84,14 +110,16 @@
         for copy in copies(i, i):
             copy.start()
 
-    rows_ref[...] = pick_rows(sizes, tokens_ref[...])
-    half = rows_ref.shape[0] // 2
+    for w in range(2):
+        rows_ref[w] = pick_rows(sizes, tokens_ref[...], w)
+    high = total_ref.shape[3]
+    tiles = block // LANES
 
     def multiply(n, w, weights):
-        columns = pl.ds(n * block if isinstance(n, int) else pl.multiple_of(n * block, LANES), block)
-        total = jnp.dot(rows_ref[...], weights, preferred_element_type=jnp.float32)
-        keep_ref[w, :, columns] = total[:half]
-        send_ref[w, :, columns] = total[half:]
+        product = jnp.dot(rows_ref[w], weights, preferred_element_type=jnp.float32)
+        for h in range(2):
+            for t in range(tiles):
+                total_ref[w, h, n * tiles + t] = product[h * high : (h + 1) * high, t * LANES : (t + 1) * LANES]
 
     for n in range(ahead):
         for w in range(2):
@@ -112,19 +140,45 @@
 
     lax.fori_loop(0, later, step, 0)
 
+    every = all_blocks * tiles
+    spans = [slice(n * tiles, (n + 1) * tiles) for n in range(all_blocks)]
+    first = lax.broadcasted_iota(jnp.int32, (tiles, high, LANES), 1) < high // 2
+    for h in range(2):
+        peaks = [jnp.zeros((high, LANES), jnp.float32)] * 2
+        for span in spans:
+            gate, up = total_ref[0, h, span], total_ref[1, h, span]
+            parts = jnp.where(first, gate, up), pltpu.roll(jnp.where(first, up, gate), high // 2, 1)
+            for i, part in enumerate(parts):
+                total_ref[i, h, span] = part
+                peaks[i] = jnp.maximum(peaks[i], jnp.max(jnp.abs(part), axis=0))
+        for i in range(2):
+            peak = jnp.broadcast_to(jnp.max(peaks[i], axis=1, keepdims=True), (high, LANES))
+            bound = jnp.maximum(peak * (1.0 + 2.0**-6), LEAST).astype(jnp.bfloat16)
+            exact = bound.astype(jnp.float32)
+            if h == i == 0:
+                keep_ref[every] = exact
+                for span in spans:
+                    keep_ref[span] = total_ref[i, h, span]
+                continue
+            send_ref = send_refs[2 * h + i - 1]
+            send_ref[every] = bound
+            for span in spans:
+                send_ref[span] = encode(total_ref[i, h, span], exact[None])
+
 
 def project(sizes, all_blocks, block, tokens, ahead, gate_weight, up_weight):
     rows, depth = tokens.shape
     width = all_blocks * block
     slots = 4
-    shape = jax.ShapeDtypeStruct((2, rows // 2, width), jnp.float32)
+    shape = (width // LANES + 1, rows // 2, LANES)
     return pl.pallas_call(
         functools.partial(project_kernel, sizes, all_blocks, block),
         in_specs=[pl.BlockSpec(memory_space=pltpu.VMEM)] * 2 + [pl.BlockSpec(memory_space=pl.ANY)] * 2,
-        out_specs=[pl.BlockSpec(memory_space=pltpu.VMEM)] * 2,
-        out_shape=[shape, shape],
+        out_specs=[pl.BlockSpec(memory_space=pltpu.VMEM)] * 4,
+        out_shape=[jax.ShapeDtypeStruct(shape, jnp.float32)] + [jax.ShapeDtypeStruct(shape, jnp.bfloat16)] * 3,
         scratch_shapes=[
-            pltpu.VMEM((rows, depth), jnp.bfloat16),
+            pltpu.VMEM((2, rows, depth), jnp.bfloat16),
+            pltpu.VMEM((2, 2, width // LANES, rows // 2, LANES), jnp.float32),
             pltpu.VMEM((slots, 2, depth, block), jnp.bfloat16),
             pltpu.SemaphoreType.DMA((slots, 2)),
         ],
@@ -135,6 +189,17 @@
     )(tokens, ahead, gate_weight, up_weight)
 
 
+def exchange(sizes, send, flip):
+    groups, gx, gy = sizes
+    pairs = [(x * gy + core, (x ^ flip(core)) * gy + core) for x in range(gx) for core in range(gy)]
+    return lax.ppermute(send, ("gx", "gy"), pairs)
+
+
+def opened(came):
+    bound = came[-1:].astype(jnp.float32)
+    return decode(came[:-1], bound), bound
+
+
 def gather_rows(sizes, tokens):
     groups, gx, gy = sizes
     both = [
@@ -153,17 +218,28 @@
     all_blocks = width // block
     ahead = fetch(all_blocks, block, min(3, all_blocks), gate_weight, up_weight)
     rows = gather_rows(sizes, tokens)
-    send, keep = project(sizes, all_blocks, block, rows, ahead, gate_weight, up_weight)
-    phases = gx.bit_length() - 1
-    for n in range(phases):
-        pairs = [
-            (x * gy + core, (x ^ masks(gx, core)[n]) * gy + core) for x in range(gx) for core in range(gy)
-        ]
-        total = keep + lax.ppermute(send, ("gx", "gy"), pairs)
-        half = total.shape[1] // 2
-        if n < phases - 1:
-            keep, send = total[:, :half], total[:, half:]
-    hidden = (jax.nn.silu(total[0]) * total[1]).astype(jnp.bfloat16)
+    keep, *sends = project(sizes, all_blocks, block, rows, ahead, gate_weight, up_weight)
+    flips = [
+        lambda core: masks(gx, core)[1],
+        lambda core: masks(gx, core)[0],
+        lambda core: masks(gx, core)[0] ^ masks(gx, core)[1],
+    ]
+    came = lax.optimization_barrier([exchange(sizes, send, flip) for send, flip in zip(sends, flips)])
+    total, bound = keep[:-1], keep[-1:]
+    for part in came:
+        value, part_bound = opened(part)
+        total, bound = total + value, bound + part_bound
+    shape = (2, total.shape[1] // 2, LANES)
+    total, bound = total.reshape(-1, *shape), bound.reshape(-1, *shape)
+    for n in range(2, gx.bit_length() - 1):
+        half = total.shape[2] // 2
+        bound = rounded_up(bound)
+        send = encode(total[:, :, half:], bound[:, :, half:])
+        send = jnp.concatenate([send, bound[:, :, half:].astype(jnp.bfloat16)], axis=0)
+        value, part_bound = opened(exchange(sizes, send, lambda core: masks(gx, core)[n]))
+        total, bound = total[:, :, :half] + value, bound[:, :, :half] + part_bound
+    hidden = (jax.nn.silu(total[:, 0]) * total[:, 1]).astype(jnp.bfloat16)
+    hidden = jnp.swapaxes(hidden, 0, 1).reshape(hidden.shape[1], width)
     each = hidden.shape[0] // groups
     own, theirs = hidden[:each], hidden[each:]
     theirs = lax.ppermute(theirs, "groups", [(g, (g + 1) % groups) for g in range(groups)])

time: 45.8 us -> 40.8 us (0.89)
  waiting for transfers between devices: 15.2 us -> 10.7 us
  starting transfers between devices: 12.4 us -> 10.9 us
  other arithmetic: 1.01 us -> 1.64 us
  Pallas kernels: 16.8 us -> 17.3 us
    ppermute x3 -> x4, waiting for transfers between devices: 13.4 us -> 8.33 us  [exchange(): return lax.ppermute(send, ('gx', 'gy'), pairs)]
    ppermute x1, starting transfers between devices: 2.78 us -> 1.55 us  [per_device(): lax.ppermute(theirs, 'groups', [(g, (g + 1) % groups) for g in range(grou...]
    ppermute x1, waiting for transfers between devices: 1.83 us -> 2.37 us  [per_device(): lax.ppermute(theirs, 'groups', [(g, (g + 1) % groups) for g in range(grou...]
    pallas_call x1, Pallas kernels: 12.5 us -> 13 us  [project(): pl.pallas_call(functools.partial(project_kernel, sizes, all_blocks, block...]
    ppermute x3 -> x4, starting transfers between devices: 6.55 us -> 6.26 us  [exchange(): return lax.ppermute(send, ('gx', 'gy'), pairs)]
  transfers between devices with their start and end apart: 7 -> 8, of which waited for: 4 -> 5; matrix products, arithmetic and copies ran while one was open for 0% -> 0% of each run, Pallas kernels for 9% -> 11%
where the time goes in v5:
time: 40.8 us; the launch traced here: 40.7 us
  Pallas kernels  17.3 us (42%)
  starting transfers between devices  10.9 us (27%)
  waiting for transfers between devices  10.7 us (26%)
  other arithmetic  1.64 us (4%)
    pallas_call x1, Pallas kernels, project(): pl.pallas_call(functools.partial(project_kernel, sizes, all_blocks, block...  13 us
    ppermute x4, waiting for transfers between devices, exchange(): return lax.ppermute(send, ('gx', 'gy'), pairs)  8.33 us
    ppermute x4, starting transfers between devices, exchange(): return lax.ppermute(send, ('gx', 'gy'), pairs)  6.26 us
    pallas_call x1, Pallas kernels, fetch(): pl.pallas_call(functools.partial(fetch_kernel, all_blocks, block), in_spe...  4.32 us
    ppermute x1, starting transfers between devices, gather_rows(): lax.ppermute(tokens, 'groups', [(g, (g + 1) % groups) for g in range(grou...  2.55 us
    ppermute x1, waiting for transfers between devices, per_device(): lax.ppermute(theirs, 'groups', [(g, (g + 1) % groups) for g in range(grou...  2.37 us
    ppermute x1, starting transfers between devices, per_device(): lax.ppermute(theirs, 'groups', [(g, (g + 1) % groups) for g in range(grou...  1.55 us
  transfers between devices with their start and end apart: 8, of which 5 were waited for; matrix products, arithmetic and copies ran while one was open for 0% of the time, Pallas kernels for 11%

profile of v5, /device:TPU:0, one launch (start us, length us, event | category | flops | bytes accessed | tf_op | source)
XLA Modules:
  0.0 40.7 jit_solution(1698552857603622656)
XLA Ops:
  0.0 0.0 copy-start
  0.0 0.5 %collective-permute-start = (bf16[4,1792]{1,0:T(4,128)(2,1)}, bf16[4,1792]{1,0:T(4,128)(2,1)S(1)}, u32[]{:S(2)}, u32[]{:S(2)}) collective-permute-start(bf16[4,1792]{1,0:T(4,128)(2,1)} %param.3), channel_id=1, source_target_pairs={{0,1},{1,0},{2,3},{3,2},{4,5},{5,4},{6,7},{7,6},{8,9},{9,8},{10,11... | collective-permute-start | bytes 43016 | tf_op jit(solution)/shard_map/ppermute | solution.py:210
  0.5 2.5 %collective-permute-start.1 = (bf16[4,1792]{1,0:T(4,128)(2,1)}, bf16[4,1792]{1,0:T(4,128)(2,1)S(1)}, u32[]{:S(2)}, u32[]{:S(2)}) collective-permute-start(bf16[4,1792]{1,0:T(4,128)(2,1)} %param.3), channel_id=1, source_target_pairs={{0,16},{16,0},{1,17},{17,1},{2,18},{18,2},{3,19},{19,3},{4,20},{20... | collective-permute-start | bytes 43016 | tf_op jit(solution)/shard_map/ppermute | solution.py:208
  3.0 0.1 collective-permute-start.2
  3.1 4.3 %shard_map.37.ahead_ref = bf16[3,2,1792,512]{3,2,1,0:T(8,128)(2,1)S(1)} custom-call(bf16[1792,13312]{1,0:T(8,128)(2,1)} %gate_hbm.3, bf16[1792,13312]{1,0:T(8,128)(2,1)} %up_hbm.3), custom_call_target="tpu_custom_call" | custom-call | bytes 11010048 | tf_op jit(solution)/shard_map/pallas_call | solution.py:64
  7.4 0.0 collective-permute-done
  7.4 0.0 collective-permute-done.1
  7.4 0.0 collective-permute-done.2
  7.5 0.0 copy-done
  7.5 13.0 %shard_map.38 = (f32[53,8,128]{2,1,0:T(8,128)S(1)}, bf16[53,8,128]{2,1,0:T(8,128)(2,1)S(1)}, bf16[53,8,128]{2,1,0:T(8,128)(2,1)S(1)}, bf16[53,8,128]{2,1,0:T(8,128)(2,1)S(1)}) custom-call(bf16[16,1792]{1,0:T(8,128)(2,1)S(1)} %pad_maximum_fusion.tokens_ref, bf16[3,2,1792,512]{3,2,1,0:T(8,128)(2,1)S(1)} %shard_map.37.ahead_ref, bf16[1792,13312]{1,0:T(8,128)(2,1)} %gate_hbm.3, ...), custom_call_target="tpu_custom_call" | custom-call | flops 763363328 | bytes 47710208 | tf_op jit(solution)/shard_map/pallas_call | solution.py:174
  20.5 1.9 %collective-permute-start.3 = (bf16[53,8,128]{2,1,0:T(8,128)(2,1)S(1)}, bf16[53,8,128]{2,1,0:T(8,128)(2,1)S(1)}, u32[]{:S(2)}, u32[]{:S(2)}) collective-permute-start(bf16[53,8,128]{2,1,0:T(8,128)(2,1)S(1)} %get-tuple-element.13), channel_id=1, source_target_pairs={{0,4},{1,3},{2,6},{3,1},{4,0},{5,7},{6,2},{7,5},{8,12},{9,11},{10,... | collective-permute-start | bytes 325640 | tf_op jit(solution)/shard_map/ppermute | solution.py:195
  22.3 1.5 %collective-permute-start.4 = (bf16[53,8,128]{2,1,0:T(8,128)(2,1)S(1)}, bf16[53,8,128]{2,1,0:T(8,128)(2,1)S(1)}, u32[]{:S(2)}, u32[]{:S(2)}) collective-permute-start(bf16[53,8,128]{2,1,0:T(8,128)(2,1)S(1)} %get-tuple-element.14), channel_id=1, source_target_pairs={{0,2},{1,5},{2,0},{3,7},{4,6},{5,1},{6,4},{7,3},{8,10},{9,13},{10,... | collective-permute-start | bytes 325640 | tf_op jit(solution)/shard_map/ppermute | solution.py:195
  23.9 0.2 collective-permute-start.5
  24.0 1.6 %collective-permute-done.3 = bf16[53,8,128]{2,1,0:T(8,128)(2,1)S(1)} collective-permute-done((bf16[53,8,128]{2,1,0:T(8,128)(2,1)S(1)}, bf16[53,8,128]{2,1,0:T(8,128)(2,1)S(1)}, u32[]{:S(2)}, u32[]{:S(2)}) %collective-permute-start.3) | collective-permute-done | bytes 108576 | tf_op jit(solution)/shard_map/ppermute | solution.py:195
  25.6 2.8 %collective-permute-done.4 = bf16[53,8,128]{2,1,0:T(8,128)(2,1)S(1)} collective-permute-done((bf16[53,8,128]{2,1,0:T(8,128)(2,1)S(1)}, bf16[53,8,128]{2,1,0:T(8,128)(2,1)S(1)}, u32[]{:S(2)}, u32[]{:S(2)}) %collective-permute-start.4) | collective-permute-done | bytes 108576 | tf_op jit(solution)/shard_map/ppermute | solution.py:195
  28.5 1.0 %collective-permute-done.5 = bf16[53,8,128]{2,1,0:T(8,128)(2,1)S(1)} collective-permute-done((bf16[53,8,128]{2,1,0:T(8,128)(2,1)S(1)}, bf16[53,8,128]{2,1,0:T(8,128)(2,1)S(1)}, u32[]{:S(2)}, u32[]{:S(2)}) %collective-permute-start.5) | collective-permute-done | bytes 108576 | tf_op jit(solution)/shard_map/ppermute | solution.py:195
  29.5 0.3 fusion.17
  29.8 0.2 fusion.24
  30.0 0.1 pad_maximum_fusion.1
  30.1 2.7 %collective-permute-start.6 = (bf16[53,2,2,128]{3,2,1,0:T(2,128)(2,1)S(1)}, bf16[53,2,2,128]{3,2,1,0:T(2,128)(2,1)S(1)}, u32[]{:S(2)}, u32[]{:S(2)}) collective-permute-start(bf16[53,2,2,128]{3,2,1,0:T(2,128)(2,1)S(1)} %pad_maximum_fusion.1), channel_id=1, source_target_pairs={{0,8},{1,9},{2,10},{3,11},{4,12},{5,13},{6,14},{7,15},{8,0},{9,1},... | collective-permute-start | bytes 162824 | tf_op jit(solution)/shard_map/ppermute | solution.py:195
  32.8 2.9 %collective-permute-done.6 = bf16[53,2,2,128]{3,2,1,0:T(2,128)(2,1)S(1)} collective-permute-done((bf16[53,2,2,128]{3,2,1,0:T(2,128)(2,1)S(1)}, bf16[53,2,2,128]{3,2,1,0:T(2,128)(2,1)S(1)}, u32[]{:S(2)}, u32[]{:S(2)}) %collective-permute-start.6) | collective-permute-done | bytes 54304 | tf_op jit(solution)/shard_map/ppermute | solution.py:195
  35.7 0.2 fusion.23
  35.9 0.1 fusion.27
  36.0 1.5 %collective-permute-start.7 = (bf16[1,6656]{1,0:T(2,128)(2,1)S(1)}, bf16[1,6656]{1,0:T(2,128)(2,1)S(1)}, u32[]{:S(2)}, u32[]{:S(2)}) collective-permute-start(bf16[1,6656]{1,0:T(2,128)(2,1)S(1)} %slice_bitcast_fusion.2), channel_id=1, source_target_pairs={{0,16},{16,0},{1,17},{17,1},{2,18},{18,2},{3,19},{19,3},{4,20},{20... | collective-permute-start | bytes 39944 | tf_op jit(solution)/shard_map/ppermute | solution.py:245
  37.6 2.4 %collective-permute-done.7 = bf16[1,6656]{1,0:T(2,128)(2,1)S(1)} collective-permute-done((bf16[1,6656]{1,0:T(2,128)(2,1)S(1)}, bf16[1,6656]{1,0:T(2,128)(2,1)S(1)}, u32[]{:S(2)}, u32[]{:S(2)}) %collective-permute-start.7) | collective-permute-done | bytes 13344 | tf_op jit(solution)/shard_map/ppermute | solution.py:245
  39.9 0.1 broadcast_select_fusion.1
  40.0 0.7 %pad_maximum_fusion.2 = bf16[1,13312]{1,0:T(2,128)(2,1)} fusion(bf16[1,6656]{1,0:T(2,128)(2,1)S(1)} %get-tuple-element.24, bf16[1,6656]{1,0:T(2,128)(2,1)S(1)} %get-tuple-element.23), kind=kLoop, calls=%fused_computation.43 | loop fusion | flops 53248 | bytes 53248 | tf_op jit(solution)/shard_map/concatenate | solution.py:247
  (6 shorter events, 0.1 us)
Async XLA Ops:
  0.0 7.5 %copy-start = (bf16[4,1792]{1,0:T(4,128)(2,1)S(1)}, bf16[4,1792]{1,0:T(4,128)(2,1)}, u32[]{:S(2)}) copy-start(bf16[4,1792]{1,0:T(4,128)(2,1)} %param.3) | copy-start | bytes 43012
  0.0 7.4 %collective-permute-start = (bf16[4,1792]{1,0:T(4,128)(2,1)}, bf16[4,1792]{1,0:T(4,128)(2,1)S(1)}, u32[]{:S(2)}, u32[]{:S(2)}) collective-permute-start(bf16[4,1792]{1,0:T(4,128)(2,1)} %param.3), channel_id=1, source_target_pairs={{0,1},{1,0},{2,3},{3,2},{4,5},{5,4},{6,7},{7,6},{8,9},{9,8},{10,11... | collective-permute-start | bytes 43016 | tf_op jit(solution)/shard_map/ppermute | solution.py:210
  0.5 7.0 %collective-permute-start.1 = (bf16[4,1792]{1,0:T(4,128)(2,1)}, bf16[4,1792]{1,0:T(4,128)(2,1)S(1)}, u32[]{:S(2)}, u32[]{:S(2)}) collective-permute-start(bf16[4,1792]{1,0:T(4,128)(2,1)} %param.3), channel_id=1, source_target_pairs={{0,16},{16,0},{1,17},{17,1},{2,18},{18,2},{3,19},{19,3},{4,20},{20... | collective-permute-start | bytes 43016 | tf_op jit(solution)/shard_map/ppermute | solution.py:208
  3.0 4.4 %collective-permute-start.2 = (bf16[4,1792]{1,0:T(4,128)(2,1)}, bf16[4,1792]{1,0:T(4,128)(2,1)S(1)}, u32[]{:S(2)}, u32[]{:S(2)}) collective-permute-start(bf16[4,1792]{1,0:T(4,128)(2,1)} %param.3), channel_id=1, source_target_pairs={{0,17},{1,16},{16,1},{17,0},{2,19},{3,18},{18,3},{19,2},{4,21},{5,... | collective-permute-start | bytes 43016 | tf_op jit(solution)/shard_map/ppermute | solution.py:209
  20.5 5.1 %collective-permute-start.3 = (bf16[53,8,128]{2,1,0:T(8,128)(2,1)S(1)}, bf16[53,8,128]{2,1,0:T(8,128)(2,1)S(1)}, u32[]{:S(2)}, u32[]{:S(2)}) collective-permute-start(bf16[53,8,128]{2,1,0:T(8,128)(2,1)S(1)} %get-tuple-element.13), channel_id=1, source_target_pairs={{0,4},{1,3},{2,6},{3,1},{4,0},{5,7},{6,2},{7,5},{8,12},{9,11},{10,... | collective-permute-start | bytes 325640 | tf_op jit(solution)/shard_map/ppermute | solution.py:195
  22.3 6.1 %collective-permute-start.4 = (bf16[53,8,128]{2,1,0:T(8,128)(2,1)S(1)}, bf16[53,8,128]{2,1,0:T(8,128)(2,1)S(1)}, u32[]{:S(2)}, u32[]{:S(2)}) collective-permute-start(bf16[53,8,128]{2,1,0:T(8,128)(2,1)S(1)} %get-tuple-element.14), channel_id=1, source_target_pairs={{0,2},{1,5},{2,0},{3,7},{4,6},{5,1},{6,4},{7,3},{8,10},{9,13},{10,... | collective-permute-start | bytes 325640 | tf_op jit(solution)/shard_map/ppermute | solution.py:195
  23.9 5.6 %collective-permute-start.5 = (bf16[53,8,128]{2,1,0:T(8,128)(2,1)S(1)}, bf16[53,8,128]{2,1,0:T(8,128)(2,1)S(1)}, u32[]{:S(2)}, u32[]{:S(2)}) collective-permute-start(bf16[53,8,128]{2,1,0:T(8,128)(2,1)S(1)} %get-tuple-element.15), channel_id=1, source_target_pairs={{0,6},{1,7},{2,4},{3,5},{4,2},{5,3},{6,0},{7,1},{8,14},{9,15},{10,... | collective-permute-start | bytes 325640 | tf_op jit(solution)/shard_map/ppermute | solution.py:195
  30.1 5.6 %collective-permute-start.6 = (bf16[53,2,2,128]{3,2,1,0:T(2,128)(2,1)S(1)}, bf16[53,2,2,128]{3,2,1,0:T(2,128)(2,1)S(1)}, u32[]{:S(2)}, u32[]{:S(2)}) collective-permute-start(bf16[53,2,2,128]{3,2,1,0:T(2,128)(2,1)S(1)} %pad_maximum_fusion.1), channel_id=1, source_target_pairs={{0,8},{1,9},{2,10},{3,11},{4,12},{5,13},{6,14},{7,15},{8,0},{9,1},... | collective-permute-start | bytes 162824 | tf_op jit(solution)/shard_map/ppermute | solution.py:195
  36.0 3.9 %collective-permute-start.7 = (bf16[1,6656]{1,0:T(2,128)(2,1)S(1)}, bf16[1,6656]{1,0:T(2,128)(2,1)S(1)}, u32[]{:S(2)}, u32[]{:S(2)}) collective-permute-start(bf16[1,6656]{1,0:T(2,128)(2,1)S(1)} %slice_bitcast_fusion.2), channel_id=1, source_target_pairs={{0,16},{16,0},{1,17},{17,1},{2,18},{18,2},{3,19},{19,3},{4,20},{20... | collective-permute-start | bytes 39944 | tf_op jit(solution)/shard_map/ppermute | solution.py:245

commit v6 on v5

--- a/solution.py
+++ b/solution.py
@@ -31,11 +31,8 @@
     return lax.reduce_precision(jnp.maximum(bound * (1.0 + 2.0**-6), LEAST), 8, 7)
 
 
-def masks(count, core):
-    bits = [1 << b for b in range(count.bit_length() - 1)]
-    if core % 2 and len(bits) > 1:
-        bits[0], bits[1] = bits[1], bits[0]
-    return bits
+def flips(core):
+    return (0, 2, 1, 3) if core % 2 else (0, 3, 2, 1)
 
 
 def column_block(width):
@@ -83,11 +80,13 @@
     source = lax.broadcasted_iota(jnp.int32, (rows, rows), 1)
     m = (place // quarter ^ w) * quarter + place % quarter
     j, q, i = m // (groups * each), (m // each) % groups, m % each
-    mine, other = masks(gx, 0), masks(gx, 1)
-    flip = jnp.zeros_like(j)
-    for n in range(len(mine)):
-        bit = (j // (1 << (len(mine) - 1 - n))) % 2
-        flip = flip + bit * jnp.where(core == 0, mine[n], other[n])
+    steps = gx // 4
+    part, flip = j // steps, jnp.zeros_like(j)
+    for n in range(1, 4):
+        flip = flip + jnp.where(part == n, jnp.where(core == 0, flips(0)[n], flips(1)[n]), 0)
+    for n in range(2, gx.bit_length() - 1):
+        steps //= 2
+        flip = flip + j // steps % 2 * (1 << n)
     row = (x ^ flip) * each + i
     wanted = (q * gy + (row // held + gy - core) % gy) * held + row % held
     pick = (source == wanted).astype(jnp.bfloat16)
@@ -219,12 +218,8 @@
     ahead = fetch(all_blocks, block, min(3, all_blocks), gate_weight, up_weight)
     rows = gather_rows(sizes, tokens)
     keep, *sends = project(sizes, all_blocks, block, rows, ahead, gate_weight, up_weight)
-    flips = [
-        lambda core: masks(gx, core)[1],
-        lambda core: masks(gx, core)[0],
-        lambda core: masks(gx, core)[0] ^ masks(gx, core)[1],
-    ]
-    came = lax.optimization_barrier([exchange(sizes, send, flip) for send, flip in zip(sends, flips)])
+    came = [exchange(sizes, send, lambda core: flips(core)[n + 1]) for n, send in enumerate(sends)]
+    came = lax.optimization_barrier(came)
     total, bound = keep[:-1], keep[-1:]
     for part in came:
         value, part_bound = opened(part)
@@ -236,7 +231,7 @@
         bound = rounded_up(bound)
         send = encode(total[:, :, half:], bound[:, :, half:])
         send = jnp.concatenate([send, bound[:, :, half:].astype(jnp.bfloat16)], axis=0)
-        value, part_bound = opened(exchange(sizes, send, lambda core: masks(gx, core)[n]))
+        value, part_bound = opened(exchange(sizes, send, lambda core: 1 << n))
         total, bound = total[:, :, :half] + value, bound[:, :, :half] + part_bound
     hidden = (jax.nn.silu(total[:, 0]) * total[:, 1]).astype(jnp.bfloat16)
     hidden = jnp.swapaxes(hidden, 0, 1).reshape(hidden.shape[1], width)

time: 40.8 us -> 40.5 us (level)
  no operation moved by 1% of the time
where the time goes in v6:
time: 40.5 us; the launch traced here: 40.4 us
  Pallas kernels  17.3 us (43%)
  starting transfers between devices  10.8 us (27%)
  waiting for transfers between devices  10.4 us (26%)
  other arithmetic  1.64 us (4%)
    pallas_call x1, Pallas kernels, project(): pl.pallas_call(functools.partial(project_kernel, sizes, all_blocks, block...  13 us
    ppermute x4, waiting for transfers between devices, exchange(): return lax.ppermute(send, ('gx', 'gy'), pairs)  8.07 us
    ppermute x4, starting transfers between devices, exchange(): return lax.ppermute(send, ('gx', 'gy'), pairs)  6.21 us
    pallas_call x1, Pallas kernels, fetch(): pl.pallas_call(functools.partial(fetch_kernel, all_blocks, block), in_spe...  4.32 us
    ppermute x1, starting transfers between devices, gather_rows(): lax.ppermute(tokens, 'groups', [(g, (g + 1) % groups) for g in range(grou...  2.55 us
    ppermute x1, waiting for transfers between devices, per_device(): lax.ppermute(theirs, 'groups', [(g, (g + 1) % groups) for g in range(grou...  2.37 us
    ppermute x1, starting transfers between devices, per_device(): lax.ppermute(theirs, 'groups', [(g, (g + 1) % groups) for g in range(grou...  1.55 us
  transfers between devices with their start and end apart: 8, of which 5 were waited for; matrix products, arithmetic and copies ran while one was open for 0% of the time, Pallas kernels for 11%

profile of v6, /device:TPU:0, one launch (start us, length us, event | category | flops | bytes accessed | tf_op | source)
XLA Modules:
  0.0 40.4 jit_solution(2630508460100234996)
XLA Ops:
  0.0 0.0 copy-start
  0.0 0.5 %collective-permute-start = (bf16[4,1792]{1,0:T(4,128)(2,1)}, bf16[4,1792]{1,0:T(4,128)(2,1)S(1)}, u32[]{:S(2)}, u32[]{:S(2)}) collective-permute-start(bf16[4,1792]{1,0:T(4,128)(2,1)} %param.3), channel_id=1, source_target_pairs={{0,1},{1,0},{2,3},{3,2},{4,5},{5,4},{6,7},{7,6},{8,9},{9,8},{10,11... | collective-permute-start | bytes 43016 | tf_op jit(solution)/shard_map/ppermute | solution.py:209
  0.5 2.5 %collective-permute-start.1 = (bf16[4,1792]{1,0:T(4,128)(2,1)}, bf16[4,1792]{1,0:T(4,128)(2,1)S(1)}, u32[]{:S(2)}, u32[]{:S(2)}) collective-permute-start(bf16[4,1792]{1,0:T(4,128)(2,1)} %param.3), channel_id=1, source_target_pairs={{0,16},{16,0},{1,17},{17,1},{2,18},{18,2},{3,19},{19,3},{4,20},{20... | collective-permute-start | bytes 43016 | tf_op jit(solution)/shard_map/ppermute | solution.py:207
  3.0 0.1 collective-permute-start.2
  3.1 4.3 %shard_map.37.ahead_ref = bf16[3,2,1792,512]{3,2,1,0:T(8,128)(2,1)S(1)} custom-call(bf16[1792,13312]{1,0:T(8,128)(2,1)} %gate_hbm.3, bf16[1792,13312]{1,0:T(8,128)(2,1)} %up_hbm.3), custom_call_target="tpu_custom_call" | custom-call | bytes 11010048 | tf_op jit(solution)/shard_map/pallas_call | solution.py:61
  7.4 0.0 collective-permute-done
  7.4 0.0 collective-permute-done.1
  7.4 0.0 collective-permute-done.2
  7.5 0.0 copy-done
  7.5 13.0 %shard_map.38 = (f32[53,8,128]{2,1,0:T(8,128)S(1)}, bf16[53,8,128]{2,1,0:T(8,128)(2,1)S(1)}, bf16[53,8,128]{2,1,0:T(8,128)(2,1)S(1)}, bf16[53,8,128]{2,1,0:T(8,128)(2,1)S(1)}) custom-call(bf16[16,1792]{1,0:T(8,128)(2,1)S(1)} %pad_maximum_fusion.tokens_ref, bf16[3,2,1792,512]{3,2,1,0:T(8,128)(2,1)S(1)} %shard_map.37.ahead_ref, bf16[1792,13312]{1,0:T(8,128)(2,1)} %gate_hbm.3, ...), custom_call_target="tpu_custom_call" | custom-call | flops 763363328 | bytes 47710208 | tf_op jit(solution)/shard_map/pallas_call | solution.py:173
  20.5 2.8 %collective-permute-start.3 = (bf16[53,8,128]{2,1,0:T(8,128)(2,1)S(1)}, bf16[53,8,128]{2,1,0:T(8,128)(2,1)S(1)}, u32[]{:S(2)}, u32[]{:S(2)}) collective-permute-start(bf16[53,8,128]{2,1,0:T(8,128)(2,1)S(1)} %get-tuple-element.13), channel_id=1, source_target_pairs={{0,6},{1,5},{2,4},{3,7},{4,2},{5,1},{6,0},{7,3},{8,14},{9,13},{10,... | collective-permute-start | bytes 325640 | tf_op jit(solution)/shard_map/ppermute | solution.py:194
  23.3 0.4 %collective-permute-start.4 = (bf16[53,8,128]{2,1,0:T(8,128)(2,1)S(1)}, bf16[53,8,128]{2,1,0:T(8,128)(2,1)S(1)}, u32[]{:S(2)}, u32[]{:S(2)}) collective-permute-start(bf16[53,8,128]{2,1,0:T(8,128)(2,1)S(1)} %get-tuple-element.14), channel_id=1, source_target_pairs={{0,4},{1,3},{2,6},{3,1},{4,0},{5,7},{6,2},{7,5},{8,12},{9,11},{10,... | collective-permute-start | bytes 325640 | tf_op jit(solution)/shard_map/ppermute | solution.py:194
  23.7 0.3 collective-permute-start.5
  24.0 3.0 %collective-permute-done.3 = bf16[53,8,128]{2,1,0:T(8,128)(2,1)S(1)} collective-permute-done((bf16[53,8,128]{2,1,0:T(8,128)(2,1)S(1)}, bf16[53,8,128]{2,1,0:T(8,128)(2,1)S(1)}, u32[]{:S(2)}, u32[]{:S(2)}) %collective-permute-start.3) | collective-permute-done | bytes 108576 | tf_op jit(solution)/shard_map/ppermute | solution.py:194
  27.0 1.8 %collective-permute-done.4 = bf16[53,8,128]{2,1,0:T(8,128)(2,1)S(1)} collective-permute-done((bf16[53,8,128]{2,1,0:T(8,128)(2,1)S(1)}, bf16[53,8,128]{2,1,0:T(8,128)(2,1)S(1)}, u32[]{:S(2)}, u32[]{:S(2)}) %collective-permute-start.4) | collective-permute-done | bytes 108576 | tf_op jit(solution)/shard_map/ppermute | solution.py:194
  28.8 0.8 %collective-permute-done.5 = bf16[53,8,128]{2,1,0:T(8,128)(2,1)S(1)} collective-permute-done((bf16[53,8,128]{2,1,0:T(8,128)(2,1)S(1)}, bf16[53,8,128]{2,1,0:T(8,128)(2,1)S(1)}, u32[]{:S(2)}, u32[]{:S(2)}) %collective-permute-start.5) | collective-permute-done | bytes 108576 | tf_op jit(solution)/shard_map/ppermute | solution.py:194
  29.7 0.3 fusion.17
  30.0 0.2 fusion.24
  30.2 0.1 pad_maximum_fusion.1
  30.3 2.7 %collective-permute-start.6 = (bf16[53,2,2,128]{3,2,1,0:T(2,128)(2,1)S(1)}, bf16[53,2,2,128]{3,2,1,0:T(2,128)(2,1)S(1)}, u32[]{:S(2)}, u32[]{:S(2)}) collective-permute-start(bf16[53,2,2,128]{3,2,1,0:T(2,128)(2,1)S(1)} %pad_maximum_fusion.1), channel_id=1, source_target_pairs={{0,8},{1,9},{2,10},{3,11},{4,12},{5,13},{6,14},{7,15},{8,0},{9,1},... | collective-permute-start | bytes 162824 | tf_op jit(solution)/shard_map/ppermute | solution.py:194
  32.9 2.5 %collective-permute-done.6 = bf16[53,2,2,128]{3,2,1,0:T(2,128)(2,1)S(1)} collective-permute-done((bf16[53,2,2,128]{3,2,1,0:T(2,128)(2,1)S(1)}, bf16[53,2,2,128]{3,2,1,0:T(2,128)(2,1)S(1)}, u32[]{:S(2)}, u32[]{:S(2)}) %collective-permute-start.6) | collective-permute-done | bytes 54304 | tf_op jit(solution)/shard_map/ppermute | solution.py:194
  35.4 0.2 fusion.23
  35.6 0.1 fusion.27
  35.7 1.5 %collective-permute-start.7 = (bf16[1,6656]{1,0:T(2,128)(2,1)S(1)}, bf16[1,6656]{1,0:T(2,128)(2,1)S(1)}, u32[]{:S(2)}, u32[]{:S(2)}) collective-permute-start(bf16[1,6656]{1,0:T(2,128)(2,1)S(1)} %slice_bitcast_fusion.2), channel_id=1, source_target_pairs={{0,16},{16,0},{1,17},{17,1},{2,18},{18,2},{3,19},{19,3},{4,20},{20... | collective-permute-start | bytes 39944 | tf_op jit(solution)/shard_map/ppermute | solution.py:240
  37.3 2.4 %collective-permute-done.7 = bf16[1,6656]{1,0:T(2,128)(2,1)S(1)} collective-permute-done((bf16[1,6656]{1,0:T(2,128)(2,1)S(1)}, bf16[1,6656]{1,0:T(2,128)(2,1)S(1)}, u32[]{:S(2)}, u32[]{:S(2)}) %collective-permute-start.7) | collective-permute-done | bytes 13344 | tf_op jit(solution)/shard_map/ppermute | solution.py:240
  39.6 0.1 broadcast_select_fusion.1
  39.7 0.7 %pad_maximum_fusion.2 = bf16[1,13312]{1,0:T(2,128)(2,1)} fusion(bf16[1,6656]{1,0:T(2,128)(2,1)S(1)} %get-tuple-element.24, bf16[1,6656]{1,0:T(2,128)(2,1)S(1)} %get-tuple-element.23), kind=kLoop, calls=%fused_computation.43 | loop fusion | flops 53248 | bytes 53248 | tf_op jit(solution)/shard_map/concatenate | solution.py:242
  (6 shorter events, 0.1 us)
Async XLA Ops:
  0.0 7.5 %copy-start = (bf16[4,1792]{1,0:T(4,128)(2,1)S(1)}, bf16[4,1792]{1,0:T(4,128)(2,1)}, u32[]{:S(2)}) copy-start(bf16[4,1792]{1,0:T(4,128)(2,1)} %param.3) | copy-start | bytes 43012
  0.0 7.4 %collective-permute-start = (bf16[4,1792]{1,0:T(4,128)(2,1)}, bf16[4,1792]{1,0:T(4,128)(2,1)S(1)}, u32[]{:S(2)}, u32[]{:S(2)}) collective-permute-start(bf16[4,1792]{1,0:T(4,128)(2,1)} %param.3), channel_id=1, source_target_pairs={{0,1},{1,0},{2,3},{3,2},{4,5},{5,4},{6,7},{7,6},{8,9},{9,8},{10,11... | collective-permute-start | bytes 43016 | tf_op jit(solution)/shard_map/ppermute | solution.py:209
  0.5 7.0 %collective-permute-start.1 = (bf16[4,1792]{1,0:T(4,128)(2,1)}, bf16[4,1792]{1,0:T(4,128)(2,1)S(1)}, u32[]{:S(2)}, u32[]{:S(2)}) collective-permute-start(bf16[4,1792]{1,0:T(4,128)(2,1)} %param.3), channel_id=1, source_target_pairs={{0,16},{16,0},{1,17},{17,1},{2,18},{18,2},{3,19},{19,3},{4,20},{20... | collective-permute-start | bytes 43016 | tf_op jit(solution)/shard_map/ppermute | solution.py:207
  3.0 4.4 %collective-permute-start.2 = (bf16[4,1792]{1,0:T(4,128)(2,1)}, bf16[4,1792]{1,0:T(4,128)(2,1)S(1)}, u32[]{:S(2)}, u32[]{:S(2)}) collective-permute-start(bf16[4,1792]{1,0:T(4,128)(2,1)} %param.3), channel_id=1, source_target_pairs={{0,17},{1,16},{16,1},{17,0},{2,19},{3,18},{18,3},{19,2},{4,21},{5,... | collective-permute-start | bytes 43016 | tf_op jit(solution)/shard_map/ppermute | solution.py:208
  20.5 6.5 %collective-permute-start.3 = (bf16[53,8,128]{2,1,0:T(8,128)(2,1)S(1)}, bf16[53,8,128]{2,1,0:T(8,128)(2,1)S(1)}, u32[]{:S(2)}, u32[]{:S(2)}) collective-permute-start(bf16[53,8,128]{2,1,0:T(8,128)(2,1)S(1)} %get-tuple-element.13), channel_id=1, source_target_pairs={{0,6},{1,5},{2,4},{3,7},{4,2},{5,1},{6,0},{7,3},{8,14},{9,13},{10,... | collective-permute-start | bytes 325640 | tf_op jit(solution)/shard_map/ppermute | solution.py:194
  23.3 5.5 %collective-permute-start.4 = (bf16[53,8,128]{2,1,0:T(8,128)(2,1)S(1)}, bf16[53,8,128]{2,1,0:T(8,128)(2,1)S(1)}, u32[]{:S(2)}, u32[]{:S(2)}) collective-permute-start(bf16[53,8,128]{2,1,0:T(8,128)(2,1)S(1)} %get-tuple-element.14), channel_id=1, source_target_pairs={{0,4},{1,3},{2,6},{3,1},{4,0},{5,7},{6,2},{7,5},{8,12},{9,11},{10,... | collective-permute-start | bytes 325640 | tf_op jit(solution)/shard_map/ppermute | solution.py:194
  23.7 5.9 %collective-permute-start.5 = (bf16[53,8,128]{2,1,0:T(8,128)(2,1)S(1)}, bf16[53,8,128]{2,1,0:T(8,128)(2,1)S(1)}, u32[]{:S(2)}, u32[]{:S(2)}) collective-permute-start(bf16[53,8,128]{2,1,0:T(8,128)(2,1)S(1)} %get-tuple-element.15), channel_id=1, source_target_pairs={{0,2},{1,7},{2,0},{3,5},{4,6},{5,3},{6,4},{7,1},{8,10},{9,15},{10,... | collective-permute-start | bytes 325640 | tf_op jit(solution)/shard_map/ppermute | solution.py:194
  30.3 5.1 %collective-permute-start.6 = (bf16[53,2,2,128]{3,2,1,0:T(2,128)(2,1)S(1)}, bf16[53,2,2,128]{3,2,1,0:T(2,128)(2,1)S(1)}, u32[]{:S(2)}, u32[]{:S(2)}) collective-permute-start(bf16[53,2,2,128]{3,2,1,0:T(2,128)(2,1)S(1)} %pad_maximum_fusion.1), channel_id=1, source_target_pairs={{0,8},{1,9},{2,10},{3,11},{4,12},{5,13},{6,14},{7,15},{8,0},{9,1},... | collective-permute-start | bytes 162824 | tf_op jit(solution)/shard_map/ppermute | solution.py:194
  35.7 3.9 %collective-permute-start.7 = (bf16[1,6656]{1,0:T(2,128)(2,1)S(1)}, bf16[1,6656]{1,0:T(2,128)(2,1)S(1)}, u32[]{:S(2)}, u32[]{:S(2)}) collective-permute-start(bf16[1,6656]{1,0:T(2,128)(2,1)S(1)} %slice_bitcast_fusion.2), channel_id=1, source_target_pairs={{0,16},{16,0},{1,17},{17,1},{2,18},{18,2},{3,19},{19,3},{4,20},{20... | collective-permute-start | bytes 39944 | tf_op jit(solution)/shard_map/ppermute | solution.py:240

commit v7 on v6

--- a/solution.py
+++ b/solution.py
@@ -31,8 +31,8 @@
     return lax.reduce_precision(jnp.maximum(bound * (1.0 + 2.0**-6), LEAST), 8, 7)
 
 
-def flips(core):
-    return (0, 2, 1, 3) if core % 2 else (0, 3, 2, 1)
+def flips():
+    return 0, 3, 2, 1
 
 
 def column_block(width):
@@ -83,7 +83,7 @@
     steps = gx // 4
     part, flip = j // steps, jnp.zeros_like(j)
     for n in range(1, 4):
-        flip = flip + jnp.where(part == n, jnp.where(core == 0, flips(0)[n], flips(1)[n]), 0)
+        flip = flip + jnp.where(part == n, flips()[n], 0)
     for n in range(2, gx.bit_length() - 1):
         steps //= 2
         flip = flip + j // steps % 2 * (1 << n)
@@ -218,7 +218,7 @@
     ahead = fetch(all_blocks, block, min(3, all_blocks), gate_weight, up_weight)
     rows = gather_rows(sizes, tokens)
     keep, *sends = project(sizes, all_blocks, block, rows, ahead, gate_weight, up_weight)
-    came = [exchange(sizes, send, lambda core: flips(core)[n + 1]) for n, send in enumerate(sends)]
+    came = [exchange(sizes, send, lambda core: flips()[n + 1]) for n, send in enumerate(sends)]
     came = lax.optimization_barrier(came)
     total, bound = keep[:-1], keep[-1:]
     for part in came:

time: 40.5 us -> 40.3 us (level)
  transfers between devices with their start and end apart: 8 -> 8, of which waited for: 5 -> 4; matrix products, arithmetic and copies ran while one was open for 0% -> 0% of each run, Pallas kernels for 11% -> 11%
where the time goes in v7:
time: 40.3 us; the launch traced here: 40.2 us
  Pallas kernels  17.3 us (43%)
  starting transfers between devices  10.8 us (27%)
  waiting for transfers between devices  10.3 us (26%)
  other arithmetic  1.64 us (4%)
    pallas_call x1, Pallas kernels, project(): pl.pallas_call(functools.partial(project_kernel, sizes, all_blocks, block...  13 us
    ppermute x4, waiting for transfers between devices, exchange(): return lax.ppermute(send, ('gx', 'gy'), pairs)  7.91 us
    ppermute x4, starting transfers between devices, exchange(): return lax.ppermute(send, ('gx', 'gy'), pairs)  6.21 us
    pallas_call x1, Pallas kernels, fetch(): pl.pallas_call(functools.partial(fetch_kernel, all_blocks, block), in_spe...  4.32 us
    ppermute x1, starting transfers between devices, gather_rows(): lax.ppermute(tokens, 'groups', [(g, (g + 1) % groups) for g in range(grou...  2.55 us
    ppermute x1, waiting for transfers between devices, per_device(): lax.ppermute(theirs, 'groups', [(g, (g + 1) % groups) for g in range(grou...  2.37 us
    ppermute x1, starting transfers between devices, per_device(): lax.ppermute(theirs, 'groups', [(g, (g + 1) % groups) for g in range(grou...  1.55 us
  transfers between devices with their start and end apart: 8, of which 4 were waited for; matrix products, arithmetic and copies ran while one was open for 0% of the time, Pallas kernels for 11%

profile of v7, /device:TPU:0, one launch (start us, length us, event | category | flops | bytes accessed | tf_op | source)
XLA Modules:
  0.0 40.2 jit_solution(9667142096636488063)
XLA Ops:
  0.0 0.0 copy-start
  0.0 0.5 %collective-permute-start = (bf16[4,1792]{1,0:T(4,128)(2,1)}, bf16[4,1792]{1,0:T(4,128)(2,1)S(1)}, u32[]{:S(2)}, u32[]{:S(2)}) collective-permute-start(bf16[4,1792]{1,0:T(4,128)(2,1)} %param.3), channel_id=1, source_target_pairs={{0,1},{1,0},{2,3},{3,2},{4,5},{5,4},{6,7},{7,6},{8,9},{9,8},{10,11... | collective-permute-start | bytes 43016 | tf_op jit(solution)/shard_map/ppermute | solution.py:209
  0.5 2.5 %collective-permute-start.1 = (bf16[4,1792]{1,0:T(4,128)(2,1)}, bf16[4,1792]{1,0:T(4,128)(2,1)S(1)}, u32[]{:S(2)}, u32[]{:S(2)}) collective-permute-start(bf16[4,1792]{1,0:T(4,128)(2,1)} %param.3), channel_id=1, source_target_pairs={{0,16},{16,0},{1,17},{17,1},{2,18},{18,2},{3,19},{19,3},{4,20},{20... | collective-permute-start | bytes 43016 | tf_op jit(solution)/shard_map/ppermute | solution.py:207
  3.0 0.1 collective-permute-start.2
  3.1 4.3 %shard_map.37.ahead_ref = bf16[3,2,1792,512]{3,2,1,0:T(8,128)(2,1)S(1)} custom-call(bf16[1792,13312]{1,0:T(8,128)(2,1)} %gate_hbm.3, bf16[1792,13312]{1,0:T(8,128)(2,1)} %up_hbm.3), custom_call_target="tpu_custom_call" | custom-call | bytes 11010048 | tf_op jit(solution)/shard_map/pallas_call | solution.py:61
  7.4 0.0 collective-permute-done
  7.4 0.0 collective-permute-done.1
  7.4 0.0 collective-permute-done.2
  7.5 0.0 copy-done
  7.5 13.0 %shard_map.38 = (f32[53,8,128]{2,1,0:T(8,128)S(1)}, bf16[53,8,128]{2,1,0:T(8,128)(2,1)S(1)}, bf16[53,8,128]{2,1,0:T(8,128)(2,1)S(1)}, bf16[53,8,128]{2,1,0:T(8,128)(2,1)S(1)}) custom-call(bf16[16,1792]{1,0:T(8,128)(2,1)S(1)} %pad_maximum_fusion.tokens_ref, bf16[3,2,1792,512]{3,2,1,0:T(8,128)(2,1)S(1)} %shard_map.37.ahead_ref, bf16[1792,13312]{1,0:T(8,128)(2,1)} %gate_hbm.3, ...), custom_call_target="tpu_custom_call" | custom-call | flops 763363328 | bytes 47710208 | tf_op jit(solution)/shard_map/pallas_call | solution.py:173
  20.5 2.8 %collective-permute-start.3 = (bf16[53,8,128]{2,1,0:T(8,128)(2,1)S(1)}, bf16[53,8,128]{2,1,0:T(8,128)(2,1)S(1)}, u32[]{:S(2)}, u32[]{:S(2)}) collective-permute-start(bf16[53,8,128]{2,1,0:T(8,128)(2,1)S(1)} %get-tuple-element.13), channel_id=1, source_target_pairs={{0,6},{1,7},{2,4},{3,5},{4,2},{5,3},{6,0},{7,1},{8,14},{9,15},{10,... | collective-permute-start | bytes 325640 | tf_op jit(solution)/shard_map/ppermute | solution.py:194
  23.3 0.4 %collective-permute-start.4 = (bf16[53,8,128]{2,1,0:T(8,128)(2,1)S(1)}, bf16[53,8,128]{2,1,0:T(8,128)(2,1)S(1)}, u32[]{:S(2)}, u32[]{:S(2)}) collective-permute-start(bf16[53,8,128]{2,1,0:T(8,128)(2,1)S(1)} %get-tuple-element.14), channel_id=1, source_target_pairs={{0,4},{1,5},{2,6},{3,7},{4,0},{5,1},{6,2},{7,3},{8,12},{9,13},{10,... | collective-permute-start | bytes 325640 | tf_op jit(solution)/shard_map/ppermute | solution.py:194
  23.7 0.3 collective-permute-start.5
  24.0 3.2 %collective-permute-done.3 = bf16[53,8,128]{2,1,0:T(8,128)(2,1)S(1)} collective-permute-done((bf16[53,8,128]{2,1,0:T(8,128)(2,1)S(1)}, bf16[53,8,128]{2,1,0:T(8,128)(2,1)S(1)}, u32[]{:S(2)}, u32[]{:S(2)}) %collective-permute-start.3) | collective-permute-done | bytes 108576 | tf_op jit(solution)/shard_map/ppermute | solution.py:194
  27.3 2.0 %collective-permute-done.4 = bf16[53,8,128]{2,1,0:T(8,128)(2,1)S(1)} collective-permute-done((bf16[53,8,128]{2,1,0:T(8,128)(2,1)S(1)}, bf16[53,8,128]{2,1,0:T(8,128)(2,1)S(1)}, u32[]{:S(2)}, u32[]{:S(2)}) %collective-permute-start.4) | collective-permute-done | bytes 108576 | tf_op jit(solution)/shard_map/ppermute | solution.py:194
  29.3 0.0 collective-permute-done.5
  29.3 0.3 fusion.17
  29.6 0.2 fusion.24
  29.9 0.1 pad_maximum_fusion.1
  29.9 2.7 %collective-permute-start.6 = (bf16[53,2,2,128]{3,2,1,0:T(2,128)(2,1)S(1)}, bf16[53,2,2,128]{3,2,1,0:T(2,128)(2,1)S(1)}, u32[]{:S(2)}, u32[]{:S(2)}) collective-permute-start(bf16[53,2,2,128]{3,2,1,0:T(2,128)(2,1)S(1)} %pad_maximum_fusion.1), channel_id=1, source_target_pairs={{0,8},{1,9},{2,10},{3,11},{4,12},{5,13},{6,14},{7,15},{8,0},{9,1},... | collective-permute-start | bytes 162824 | tf_op jit(solution)/shard_map/ppermute | solution.py:194
  32.6 2.6 %collective-permute-done.6 = bf16[53,2,2,128]{3,2,1,0:T(2,128)(2,1)S(1)} collective-permute-done((bf16[53,2,2,128]{3,2,1,0:T(2,128)(2,1)S(1)}, bf16[53,2,2,128]{3,2,1,0:T(2,128)(2,1)S(1)}, u32[]{:S(2)}, u32[]{:S(2)}) %collective-permute-start.6) | collective-permute-done | bytes 54304 | tf_op jit(solution)/shard_map/ppermute | solution.py:194
  35.2 0.2 fusion.23
  35.4 0.1 fusion.27
  35.6 1.5 %collective-permute-start.7 = (bf16[1,6656]{1,0:T(2,128)(2,1)S(1)}, bf16[1,6656]{1,0:T(2,128)(2,1)S(1)}, u32[]{:S(2)}, u32[]{:S(2)}) collective-permute-start(bf16[1,6656]{1,0:T(2,128)(2,1)S(1)} %slice_bitcast_fusion.2), channel_id=1, source_target_pairs={{0,16},{16,0},{1,17},{17,1},{2,18},{18,2},{3,19},{19,3},{4,20},{20... | collective-permute-start | bytes 39944 | tf_op jit(solution)/shard_map/ppermute | solution.py:240
  37.1 2.4 %collective-permute-done.7 = bf16[1,6656]{1,0:T(2,128)(2,1)S(1)} collective-permute-done((bf16[1,6656]{1,0:T(2,128)(2,1)S(1)}, bf16[1,6656]{1,0:T(2,128)(2,1)S(1)}, u32[]{:S(2)}, u32[]{:S(2)}) %collective-permute-start.7) | collective-permute-done | bytes 13344 | tf_op jit(solution)/shard_map/ppermute | solution.py:240
  39.5 0.1 broadcast_select_fusion.1
  39.5 0.7 %pad_maximum_fusion.2 = bf16[1,13312]{1,0:T(2,128)(2,1)} fusion(bf16[1,6656]{1,0:T(2,128)(2,1)S(1)} %get-tuple-element.24, bf16[1,6656]{1,0:T(2,128)(2,1)S(1)} %get-tuple-element.23), kind=kLoop, calls=%fused_computation.43 | loop fusion | flops 53248 | bytes 53248 | tf_op jit(solution)/shard_map/concatenate | solution.py:242
  (6 shorter events, 0.1 us)
Async XLA Ops:
  0.0 7.5 %copy-start = (bf16[4,1792]{1,0:T(4,128)(2,1)S(1)}, bf16[4,1792]{1,0:T(4,128)(2,1)}, u32[]{:S(2)}) copy-start(bf16[4,1792]{1,0:T(4,128)(2,1)} %param.3) | copy-start | bytes 43012
  0.0 7.4 %collective-permute-start = (bf16[4,1792]{1,0:T(4,128)(2,1)}, bf16[4,1792]{1,0:T(4,128)(2,1)S(1)}, u32[]{:S(2)}, u32[]{:S(2)}) collective-permute-start(bf16[4,1792]{1,0:T(4,128)(2,1)} %param.3), channel_id=1, source_target_pairs={{0,1},{1,0},{2,3},{3,2},{4,5},{5,4},{6,7},{7,6},{8,9},{9,8},{10,11... | collective-permute-start | bytes 43016 | tf_op jit(solution)/shard_map/ppermute | solution.py:209
  0.5 7.0 %collective-permute-start.1 = (bf16[4,1792]{1,0:T(4,128)(2,1)}, bf16[4,1792]{1,0:T(4,128)(2,1)S(1)}, u32[]{:S(2)}, u32[]{:S(2)}) collective-permute-start(bf16[4,1792]{1,0:T(4,128)(2,1)} %param.3), channel_id=1, source_target_pairs={{0,16},{16,0},{1,17},{17,1},{2,18},{18,2},{3,19},{19,3},{4,20},{20... | collective-permute-start | bytes 43016 | tf_op jit(solution)/shard_map/ppermute | solution.py:207
  3.0 4.4 %collective-permute-start.2 = (bf16[4,1792]{1,0:T(4,128)(2,1)}, bf16[4,1792]{1,0:T(4,128)(2,1)S(1)}, u32[]{:S(2)}, u32[]{:S(2)}) collective-permute-start(bf16[4,1792]{1,0:T(4,128)(2,1)} %param.3), channel_id=1, source_target_pairs={{0,17},{1,16},{16,1},{17,0},{2,19},{3,18},{18,3},{19,2},{4,21},{5,... | collective-permute-start | bytes 43016 | tf_op jit(solution)/shard_map/ppermute | solution.py:208
  20.5 6.8 %collective-permute-start.3 = (bf16[53,8,128]{2,1,0:T(8,128)(2,1)S(1)}, bf16[53,8,128]{2,1,0:T(8,128)(2,1)S(1)}, u32[]{:S(2)}, u32[]{:S(2)}) collective-permute-start(bf16[53,8,128]{2,1,0:T(8,128)(2,1)S(1)} %get-tuple-element.13), channel_id=1, source_target_pairs={{0,6},{1,7},{2,4},{3,5},{4,2},{5,3},{6,0},{7,1},{8,14},{9,15},{10,... | collective-permute-start | bytes 325640 | tf_op jit(solution)/shard_map/ppermute | solution.py:194
  23.3 6.0 %collective-permute-start.4 = (bf16[53,8,128]{2,1,0:T(8,128)(2,1)S(1)}, bf16[53,8,128]{2,1,0:T(8,128)(2,1)S(1)}, u32[]{:S(2)}, u32[]{:S(2)}) collective-permute-start(bf16[53,8,128]{2,1,0:T(8,128)(2,1)S(1)} %get-tuple-element.14), channel_id=1, source_target_pairs={{0,4},{1,5},{2,6},{3,7},{4,0},{5,1},{6,2},{7,3},{8,12},{9,13},{10,... | collective-permute-start | bytes 325640 | tf_op jit(solution)/shard_map/ppermute | solution.py:194
  23.7 5.6 %collective-permute-start.5 = (bf16[53,8,128]{2,1,0:T(8,128)(2,1)S(1)}, bf16[53,8,128]{2,1,0:T(8,128)(2,1)S(1)}, u32[]{:S(2)}, u32[]{:S(2)}) collective-permute-start(bf16[53,8,128]{2,1,0:T(8,128)(2,1)S(1)} %get-tuple-element.15), channel_id=1, source_target_pairs={{0,2},{1,3},{2,0},{3,1},{4,6},{5,7},{6,4},{7,5},{8,10},{9,11},{10,... | collective-permute-start | bytes 325640 | tf_op jit(solution)/shard_map/ppermute | solution.py:194
  29.9 5.3 %collective-permute-start.6 = (bf16[53,2,2,128]{3,2,1,0:T(2,128)(2,1)S(1)}, bf16[53,2,2,128]{3,2,1,0:T(2,128)(2,1)S(1)}, u32[]{:S(2)}, u32[]{:S(2)}) collective-permute-start(bf16[53,2,2,128]{3,2,1,0:T(2,128)(2,1)S(1)} %pad_maximum_fusion.1), channel_id=1, source_target_pairs={{0,8},{1,9},{2,10},{3,11},{4,12},{5,13},{6,14},{7,15},{8,0},{9,1},... | collective-permute-start | bytes 162824 | tf_op jit(solution)/shard_map/ppermute | solution.py:194
  35.6 3.9 %collective-permute-start.7 = (bf16[1,6656]{1,0:T(2,128)(2,1)S(1)}, bf16[1,6656]{1,0:T(2,128)(2,1)S(1)}, u32[]{:S(2)}, u32[]{:S(2)}) collective-permute-start(bf16[1,6656]{1,0:T(2,128)(2,1)S(1)} %slice_bitcast_fusion.2), channel_id=1, source_target_pairs={{0,16},{16,0},{1,17},{17,1},{2,18},{18,2},{3,19},{19,3},{4,20},{20... | collective-permute-start | bytes 39944 | tf_op jit(solution)/shard_map/ppermute | solution.py:240

commit v8 on v7

--- a/solution.py
+++ b/solution.py
@@ -75,10 +75,13 @@
     rows = tokens.shape[0]
     each = rows // (groups * gx)
     held = rows // (groups * gy)
-    quarter = rows // 4
+    quarter, unit = rows // 4, groups * each
     place = lax.broadcasted_iota(jnp.int32, (rows, rows), 0)
     source = lax.broadcasted_iota(jnp.int32, (rows, rows), 1)
-    m = (place // quarter ^ w) * quarter + place % quarter
+    odd = (place // unit) % 2 ^ w
+    count = quarter // unit
+    step = (place % (2 * quarter) // (2 * unit) + count - odd * w) % count
+    m = (place // (2 * quarter) * 2 + odd) * quarter + step * unit + place % unit
     j, q, i = m // (groups * each), (m // each) % groups, m % each
     steps = gx // 4
     part, flip = j // steps, jnp.zeros_like(j)
@@ -120,11 +123,25 @@
             for t in range(tiles):
                 total_ref[w, h, n * tiles + t] = product[h * high : (h + 1) * high, t * LANES : (t + 1) * LANES]
 
+    unit = sizes[0] * (2 * high // (sizes[0] * sizes[1]))
+    first = lax.broadcasted_iota(jnp.int32, (tiles, high, LANES), 1) // unit % 2 == 0
+
+    def arrange(n, peaks):
+        span = pl.ds(n * tiles, tiles)
+        peaks = list(peaks)
+        for h in range(2):
+            gate, up = total_ref[0, h, span], total_ref[1, h, span]
+            parts = jnp.where(first, gate, up), pltpu.roll(jnp.where(first, up, gate), high - unit, 1)
+            for i, part in enumerate(parts):
+                total_ref[i, h, span] = part
+                peaks[2 * h + i] = jnp.maximum(peaks[2 * h + i], jnp.max(jnp.abs(part), axis=0))
+        return tuple(peaks)
+
     for n in range(ahead):
         for w in range(2):
             multiply(n, w, ahead_ref[n, w])
 
-    def step(n, carry):
+    def step(n, peaks):
         slot = lax.rem(n, slots)
 
         @pl.when(n + slots - 1 < later)
@@ -132,37 +149,34 @@
             for copy in copies(n + slots - 1, lax.rem(n + slots - 1, slots)):
                 copy.start()
 
+        peaks = arrange(ahead + n - 1, peaks)
         for w, copy in enumerate(copies(n, slot)):
             copy.wait()
             multiply(ahead + n, w, buffer[slot, w])
-        return carry
-
-    lax.fori_loop(0, later, step, 0)
+        return peaks
+
+    peaks = (jnp.zeros((high, LANES), jnp.float32),) * 4
+    for n in range(ahead - 1):
+        peaks = arrange(n, peaks)
+    peaks = lax.fori_loop(0, later, step, peaks)
+    peaks = arrange(all_blocks - 1, peaks)
 
     every = all_blocks * tiles
-    spans = [slice(n * tiles, (n + 1) * tiles) for n in range(all_blocks)]
-    first = lax.broadcasted_iota(jnp.int32, (tiles, high, LANES), 1) < high // 2
-    for h in range(2):
-        peaks = [jnp.zeros((high, LANES), jnp.float32)] * 2
-        for span in spans:
-            gate, up = total_ref[0, h, span], total_ref[1, h, span]
-            parts = jnp.where(first, gate, up), pltpu.roll(jnp.where(first, up, gate), high // 2, 1)
-            for i, part in enumerate(parts):
-                total_ref[i, h, span] = part
-                peaks[i] = jnp.maximum(peaks[i], jnp.max(jnp.abs(part), axis=0))
-        for i in range(2):
-            peak = jnp.broadcast_to(jnp.max(peaks[i], axis=1, keepdims=True), (high, LANES))
-            bound = jnp.maximum(peak * (1.0 + 2.0**-6), LEAST).astype(jnp.bfloat16)
-            exact = bound.astype(jnp.float32)
-            if h == i == 0:
-                keep_ref[every] = exact
-                for span in spans:
-                    keep_ref[span] = total_ref[i, h, span]
-                continue
-            send_ref = send_refs[2 * h + i - 1]
-            send_ref[every] = bound
-            for span in spans:
-                send_ref[span] = encode(total_ref[i, h, span], exact[None])
+    for i in range(4):
+        done_ref = total_ref.at[i % 2, i // 2]
+        peak = jnp.broadcast_to(jnp.max(peaks[i], axis=1, keepdims=True), (high, LANES))
+        bound = jnp.maximum(peak * (1.0 + 2.0**-6), LEAST).astype(jnp.bfloat16)
+        exact = bound.astype(jnp.float32)
+        if i == 0:
+            keep_ref[every] = exact
+        else:
+            send_refs[i - 1][every] = bound
+        for n in range(all_blocks):
+            span = slice(n * tiles, (n + 1) * tiles)
+            if i == 0:
+                keep_ref[span] = done_ref[span]
+            else:
+                send_refs[i - 1][span] = encode(done_ref[span], exact[None])
 
 
 def project(sizes, all_blocks, block, tokens, ahead, gate_weight, up_weight):
@@ -195,8 +209,15 @@
 
 
 def opened(came):
-    bound = came[-1:].astype(jnp.float32)
-    return decode(came[:-1], bound), bound
+    plain = came.astype(jnp.float32)
+    last = lax.broadcasted_iota(jnp.int32, came.shape, 0) == came.shape[0] - 1
+    return jnp.where(last, plain, decode(came, plain[-1:]))
+
+
+def coded(sums, bound):
+    bound = rounded_up(bound)
+    last = lax.broadcasted_iota(jnp.int32, sums.shape, 0) == sums.shape[0] - 1
+    return jnp.where(last, jnp.broadcast_to(bound, sums.shape).astype(jnp.bfloat16), encode(sums, bound))
 
 
 def gather_rows(sizes, tokens):
@@ -219,21 +240,21 @@
     rows = gather_rows(sizes, tokens)
     keep, *sends = project(sizes, all_blocks, block, rows, ahead, gate_weight, up_weight)
     came = [exchange(sizes, send, lambda core: flips()[n + 1]) for n, send in enumerate(sends)]
-    came = lax.optimization_barrier(came)
-    total, bound = keep[:-1], keep[-1:]
-    for part in came:
-        value, part_bound = opened(part)
-        total, bound = total + value, bound + part_bound
-    shape = (2, total.shape[1] // 2, LANES)
-    total, bound = total.reshape(-1, *shape), bound.reshape(-1, *shape)
+    keep, *came = lax.optimization_barrier((keep, *came))
+    parts = [keep, *came]
     for n in range(2, gx.bit_length() - 1):
-        half = total.shape[2] // 2
-        bound = rounded_up(bound)
-        send = encode(total[:, :, half:], bound[:, :, half:])
-        send = jnp.concatenate([send, bound[:, :, half:].astype(jnp.bfloat16)], axis=0)
-        value, part_bound = opened(exchange(sizes, send, lambda core: 1 << n))
-        total, bound = total[:, :, :half] + value, bound[:, :, :half] + part_bound
-    hidden = (jax.nn.silu(total[:, 0]) * total[:, 1]).astype(jnp.bfloat16)
+        half = parts[0].shape[1] // 2
+        send = [part[:, half:] for part in parts]
+        bound = sum(part[-1:].astype(jnp.float32) for part in send)
+        send = coded(sum((opened(part) for part in send[1:]), send[0]), bound)
+        send, *parts = lax.optimization_barrier((send, *parts))
+        came = exchange(sizes, send, lambda core: 1 << n)
+        keep = [part[:, :half] for part in parts]
+        keep = sum((opened(part) for part in keep[1:]), keep[0])
+        parts = lax.optimization_barrier((keep, came))
+    total = sum((opened(part) for part in parts[1:]), parts[0])[:-1]
+    half = total.shape[1] // 2
+    hidden = (jax.nn.silu(total[:, :half]) * total[:, half:]).astype(jnp.bfloat16)
     hidden = jnp.swapaxes(hidden, 0, 1).reshape(hidden.shape[1], width)
     each = hidden.shape[0] // groups
     own, theirs = hidden[:each], hidden[each:]

time: 40.3 us -> 40.3 us (level)
    select_n x0 -> x1, other arithmetic: none -> 0.48 us  [coded(): jnp.where(last, jnp.broadcast_to(bound, sums.shape).astype(jnp.bfloat16),...]
  transfers between devices with their start and end apart: 8 -> 8, of which waited for: 4 -> 4; matrix products, arithmetic and copies ran while one was open for 0% -> 1% of each run, Pallas kernels for 11% -> 11%
where the time goes in v8:
time: 40.3 us; the launch traced here: 40.2 us
  Pallas kernels  17.2 us (43%)
  starting transfers between devices  10.8 us (27%)
  waiting for transfers between devices  9.96 us (25%)
  other arithmetic  1.95 us (5%)
    pallas_call x1, Pallas kernels, project(): pl.pallas_call(functools.partial(project_kernel, sizes, all_blocks, block...  12.9 us
    ppermute x4, waiting for transfers between devices, exchange(): return lax.ppermute(send, ('gx', 'gy'), pairs)  7.58 us
    ppermute x4, starting transfers between devices, exchange(): return lax.ppermute(send, ('gx', 'gy'), pairs)  6.21 us
    pallas_call x1, Pallas kernels, fetch(): pl.pallas_call(functools.partial(fetch_kernel, all_blocks, block), in_spe...  4.32 us
    ppermute x1, starting transfers between devices, gather_rows(): lax.ppermute(tokens, 'groups', [(g, (g + 1) % groups) for g in range(grou...  2.55 us
    ppermute x1, waiting for transfers between devices, per_device(): lax.ppermute(theirs, 'groups', [(g, (g + 1) % groups) for g in range(grou...  2.37 us
    ppermute x1, starting transfers between devices, per_device(): lax.ppermute(theirs, 'groups', [(g, (g + 1) % groups) for g in range(grou...  1.55 us
  transfers between devices with their start and end apart: 8, of which 4 were waited for; matrix products, arithmetic and copies ran while one was open for 1% of the time, Pallas kernels for 11%

profile of v8, /device:TPU:0, one launch (start us, length us, event | category | flops | bytes accessed | tf_op | source)
XLA Modules:
  0.0 40.2 jit_solution(12161083966556164660)
XLA Ops:
  0.0 0.0 copy-start
  0.0 0.5 %collective-permute-start = (bf16[4,1792]{1,0:T(4,128)(2,1)}, bf16[4,1792]{1,0:T(4,128)(2,1)S(1)}, u32[]{:S(2)}, u32[]{:S(2)}) collective-permute-start(bf16[4,1792]{1,0:T(4,128)(2,1)} %param.3), channel_id=1, source_target_pairs={{0,1},{1,0},{2,3},{3,2},{4,5},{5,4},{6,7},{7,6},{8,9},{9,8},{10,11... | collective-permute-start | bytes 43016 | tf_op jit(solution)/shard_map/ppermute | solution.py:230
  0.5 2.5 %collective-permute-start.1 = (bf16[4,1792]{1,0:T(4,128)(2,1)}, bf16[4,1792]{1,0:T(4,128)(2,1)S(1)}, u32[]{:S(2)}, u32[]{:S(2)}) collective-permute-start(bf16[4,1792]{1,0:T(4,128)(2,1)} %param.3), channel_id=1, source_target_pairs={{0,16},{16,0},{1,17},{17,1},{2,18},{18,2},{3,19},{19,3},{4,20},{20... | collective-permute-start | bytes 43016 | tf_op jit(solution)/shard_map/ppermute | solution.py:228
  3.0 0.1 collective-permute-start.2
  3.1 4.3 %shard_map.37.ahead_ref = bf16[3,2,1792,512]{3,2,1,0:T(8,128)(2,1)S(1)} custom-call(bf16[1792,13312]{1,0:T(8,128)(2,1)} %gate_hbm.3, bf16[1792,13312]{1,0:T(8,128)(2,1)} %up_hbm.3), custom_call_target="tpu_custom_call" | custom-call | bytes 11010048 | tf_op jit(solution)/shard_map/pallas_call | solution.py:61
  7.4 0.0 collective-permute-done
  7.4 0.0 collective-permute-done.1
  7.4 0.0 collective-permute-done.2
  7.5 0.0 copy-done
  7.5 12.9 %shard_map.38 = (f32[53,8,128]{2,1,0:T(8,128)S(1)}, bf16[53,8,128]{2,1,0:T(8,128)(2,1)S(1)}, bf16[53,8,128]{2,1,0:T(8,128)(2,1)S(1)}, bf16[53,8,128]{2,1,0:T(8,128)(2,1)S(1)}) custom-call(bf16[16,1792]{1,0:T(8,128)(2,1)S(1)} %pad_maximum_fusion.tokens_ref, bf16[3,2,1792,512]{3,2,1,0:T(8,128)(2,1)S(1)} %shard_map.37.ahead_ref, bf16[1792,13312]{1,0:T(8,128)(2,1)} %gate_hbm.3, ...), custom_call_target="tpu_custom_call" | custom-call | flops 763363328 | bytes 47710208 | tf_op jit(solution)/shard_map/pallas_call | solution.py:187
  20.4 2.8 %collective-permute-start.3 = (bf16[53,8,128]{2,1,0:T(8,128)(2,1)S(1)}, bf16[53,8,128]{2,1,0:T(8,128)(2,1)S(1)}, u32[]{:S(2)}, u32[]{:S(2)}) collective-permute-start(bf16[53,8,128]{2,1,0:T(8,128)(2,1)S(1)} %get-tuple-element.21), channel_id=1, source_target_pairs={{0,6},{1,7},{2,4},{3,5},{4,2},{5,3},{6,0},{7,1},{8,14},{9,15},{10,... | collective-permute-start | bytes 325640 | tf_op jit(solution)/shard_map/ppermute | solution.py:208
  23.2 0.4 %collective-permute-start.4 = (bf16[53,8,128]{2,1,0:T(8,128)(2,1)S(1)}, bf16[53,8,128]{2,1,0:T(8,128)(2,1)S(1)}, u32[]{:S(2)}, u32[]{:S(2)}) collective-permute-start(bf16[53,8,128]{2,1,0:T(8,128)(2,1)S(1)} %get-tuple-element.22), channel_id=1, source_target_pairs={{0,4},{1,5},{2,6},{3,7},{4,0},{5,1},{6,2},{7,3},{8,12},{9,13},{10,... | collective-permute-start | bytes 325640 | tf_op jit(solution)/shard_map/ppermute | solution.py:208
  23.7 0.3 collective-permute-start.5
  24.0 3.2 %collective-permute-done.3 = bf16[53,8,128]{2,1,0:T(8,128)(2,1)S(1)} collective-permute-done((bf16[53,8,128]{2,1,0:T(8,128)(2,1)S(1)}, bf16[53,8,128]{2,1,0:T(8,128)(2,1)S(1)}, u32[]{:S(2)}, u32[]{:S(2)}) %collective-permute-start.3) | collective-permute-done | bytes 108576 | tf_op jit(solution)/shard_map/ppermute | solution.py:208
  27.2 2.1 %collective-permute-done.4 = bf16[53,8,128]{2,1,0:T(8,128)(2,1)S(1)} collective-permute-done((bf16[53,8,128]{2,1,0:T(8,128)(2,1)S(1)}, bf16[53,8,128]{2,1,0:T(8,128)(2,1)S(1)}, u32[]{:S(2)}, u32[]{:S(2)}) %collective-permute-start.4) | collective-permute-done | bytes 108576 | tf_op jit(solution)/shard_map/ppermute | solution.py:208
  29.2 0.0 collective-permute-done.5
  29.4 0.5 %broadcast_select_fusion = bf16[53,4,128]{2,1,0:T(4,128)(2,1)S(1)} fusion(pred[53]{0:T(512)(128)(4,1)S(1)} %iota_compare_fusion, f32[4,128]{1,0:T(4,128)S(1)} %get-tuple-element.42, f32[4,128]{1,0:T(4,128)S(1)} %fusion.22, f32[4,128]{1,0:T(4,128)S(1)} %fusion.23, f32[4,128]{1,0:T(4,128)S(1)} %get-tuple-element.41, f32[53,8,128]{2,1,0:T(8,128)S(1)} %get-tuple-element.28, ...), kind=kLoop, calls=%fused_computation.30 | loop fusion | flops 1193984 | bytes 334901 | tf_op jit(solution)/shard_map/jit(_where)/select_n | solution.py:220
  30.0 2.7 %collective-permute-start.6 = (bf16[53,4,128]{2,1,0:T(4,128)(2,1)S(1)}, bf16[53,4,128]{2,1,0:T(4,128)(2,1)S(1)}, u32[]{:S(2)}, u32[]{:S(2)}) collective-permute-start(bf16[53,4,128]{2,1,0:T(4,128)(2,1)S(1)} %broadcast_select_fusion), channel_id=1, source_target_pairs={{0,8},{1,9},{2,10},{3,11},{4,12},{5,13},{6,14},{7,15},{8,0},{9,1},... | collective-permute-start | bytes 162824 | tf_op jit(solution)/shard_map/ppermute | solution.py:208
  32.6 0.3 fusion.10
  32.9 2.3 %collective-permute-done.6 = bf16[53,4,128]{2,1,0:T(4,128)(2,1)S(1)} collective-permute-done((bf16[53,4,128]{2,1,0:T(4,128)(2,1)S(1)}, bf16[53,4,128]{2,1,0:T(4,128)(2,1)S(1)}, u32[]{:S(2)}, u32[]{:S(2)}) %collective-permute-start.6) | collective-permute-done | bytes 54304 | tf_op jit(solution)/shard_map/ppermute | solution.py:208
  35.3 0.1 fusion.14
  35.4 0.1 fusion.17
  35.5 1.5 %collective-permute-start.7 = (bf16[1,6656]{1,0:T(2,128)(2,1)S(1)}, bf16[1,6656]{1,0:T(2,128)(2,1)S(1)}, u32[]{:S(2)}, u32[]{:S(2)}) collective-permute-start(bf16[1,6656]{1,0:T(2,128)(2,1)S(1)} %slice_bitcast_fusion), channel_id=1, source_target_pairs={{0,16},{16,0},{1,17},{17,1},{2,18},{18,2},{3,19},{19,3},{4,20},{20... | collective-permute-start | bytes 39944 | tf_op jit(solution)/shard_map/ppermute | solution.py:261
  37.1 2.4 %collective-permute-done.7 = bf16[1,6656]{1,0:T(2,128)(2,1)S(1)} collective-permute-done((bf16[1,6656]{1,0:T(2,128)(2,1)S(1)}, bf16[1,6656]{1,0:T(2,128)(2,1)S(1)}, u32[]{:S(2)}, u32[]{:S(2)}) %collective-permute-start.7) | collective-permute-done | bytes 13344 | tf_op jit(solution)/shard_map/ppermute | solution.py:261
  39.5 0.1 broadcast_select_fusion.2
  39.5 0.7 %pad_maximum_fusion.1 = bf16[1,13312]{1,0:T(2,128)(2,1)} fusion(bf16[1,6656]{1,0:T(2,128)(2,1)S(1)} %get-tuple-element.38, bf16[1,6656]{1,0:T(2,128)(2,1)S(1)} %get-tuple-element.37), kind=kLoop, calls=%fused_computation.33 | loop fusion | flops 53248 | bytes 53248 | tf_op jit(solution)/shard_map/concatenate | solution.py:263
  (17 shorter events, 0.3 us)
Async XLA Ops:
  0.0 7.5 %copy-start = (bf16[4,1792]{1,0:T(4,128)(2,1)S(1)}, bf16[4,1792]{1,0:T(4,128)(2,1)}, u32[]{:S(2)}) copy-start(bf16[4,1792]{1,0:T(4,128)(2,1)} %param.3) | copy-start | bytes 43012
  0.0 7.4 %collective-permute-start = (bf16[4,1792]{1,0:T(4,128)(2,1)}, bf16[4,1792]{1,0:T(4,128)(2,1)S(1)}, u32[]{:S(2)}, u32[]{:S(2)}) collective-permute-start(bf16[4,1792]{1,0:T(4,128)(2,1)} %param.3), channel_id=1, source_target_pairs={{0,1},{1,0},{2,3},{3,2},{4,5},{5,4},{6,7},{7,6},{8,9},{9,8},{10,11... | collective-permute-start | bytes 43016 | tf_op jit(solution)/shard_map/ppermute | solution.py:230
  0.5 7.0 %collective-permute-start.1 = (bf16[4,1792]{1,0:T(4,128)(2,1)}, bf16[4,1792]{1,0:T(4,128)(2,1)S(1)}, u32[]{:S(2)}, u32[]{:S(2)}) collective-permute-start(bf16[4,1792]{1,0:T(4,128)(2,1)} %param.3), channel_id=1, source_target_pairs={{0,16},{16,0},{1,17},{17,1},{2,18},{18,2},{3,19},{19,3},{4,20},{20... | collective-permute-start | bytes 43016 | tf_op jit(solution)/shard_map/ppermute | solution.py:228
  3.0 4.4 %collective-permute-start.2 = (bf16[4,1792]{1,0:T(4,128)(2,1)}, bf16[4,1792]{1,0:T(4,128)(2,1)S(1)}, u32[]{:S(2)}, u32[]{:S(2)}) collective-permute-start(bf16[4,1792]{1,0:T(4,128)(2,1)} %param.3), channel_id=1, source_target_pairs={{0,17},{1,16},{16,1},{17,0},{2,19},{3,18},{18,3},{19,2},{4,21},{5,... | collective-permute-start | bytes 43016 | tf_op jit(solution)/shard_map/ppermute | solution.py:229
  20.4 6.8 %collective-permute-start.3 = (bf16[53,8,128]{2,1,0:T(8,128)(2,1)S(1)}, bf16[53,8,128]{2,1,0:T(8,128)(2,1)S(1)}, u32[]{:S(2)}, u32[]{:S(2)}) collective-permute-start(bf16[53,8,128]{2,1,0:T(8,128)(2,1)S(1)} %get-tuple-element.21), channel_id=1, source_target_pairs={{0,6},{1,7},{2,4},{3,5},{4,2},{5,3},{6,0},{7,1},{8,14},{9,15},{10,... | collective-permute-start | bytes 325640 | tf_op jit(solution)/shard_map/ppermute | solution.py:208
  23.2 6.0 %collective-permute-start.4 = (bf16[53,8,128]{2,1,0:T(8,128)(2,1)S(1)}, bf16[53,8,128]{2,1,0:T(8,128)(2,1)S(1)}, u32[]{:S(2)}, u32[]{:S(2)}) collective-permute-start(bf16[53,8,128]{2,1,0:T(8,128)(2,1)S(1)} %get-tuple-element.22), channel_id=1, source_target_pairs={{0,4},{1,5},{2,6},{3,7},{4,0},{5,1},{6,2},{7,3},{8,12},{9,13},{10,... | collective-permute-start | bytes 325640 | tf_op jit(solution)/shard_map/ppermute | solution.py:208
  23.7 5.6 %collective-permute-start.5 = (bf16[53,8,128]{2,1,0:T(8,128)(2,1)S(1)}, bf16[53,8,128]{2,1,0:T(8,128)(2,1)S(1)}, u32[]{:S(2)}, u32[]{:S(2)}) collective-permute-start(bf16[53,8,128]{2,1,0:T(8,128)(2,1)S(1)} %get-tuple-element.23), channel_id=1, source_target_pairs={{0,2},{1,3},{2,0},{3,1},{4,6},{5,7},{6,4},{7,5},{8,10},{9,11},{10,... | collective-permute-start | bytes 325640 | tf_op jit(solution)/shard_map/ppermute | solution.py:208
  30.0 5.3 %collective-permute-start.6 = (bf16[53,4,128]{2,1,0:T(4,128)(2,1)S(1)}, bf16[53,4,128]{2,1,0:T(4,128)(2,1)S(1)}, u32[]{:S(2)}, u32[]{:S(2)}) collective-permute-start(bf16[53,4,128]{2,1,0:T(4,128)(2,1)S(1)} %broadcast_select_fusion), channel_id=1, source_target_pairs={{0,8},{1,9},{2,10},{3,11},{4,12},{5,13},{6,14},{7,15},{8,0},{9,1},... | collective-permute-start | bytes 162824 | tf_op jit(solution)/shard_map/ppermute | solution.py:208
  35.5 3.9 %collective-permute-start.7 = (bf16[1,6656]{1,0:T(2,128)(2,1)S(1)}, bf16[1,6656]{1,0:T(2,128)(2,1)S(1)}, u32[]{:S(2)}, u32[]{:S(2)}) collective-permute-start(bf16[1,6656]{1,0:T(2,128)(2,1)S(1)} %slice_bitcast_fusion), channel_id=1, source_target_pairs={{0,16},{16,0},{1,17},{17,1},{2,18},{18,2},{3,19},{19,3},{4,20},{20... | collective-permute-start | bytes 39944 | tf_op jit(solution)/shard_map/ppermute | solution.py:261
